TPU v7x, 128 devices: a whole 4x4x4 slice. The times are simulated.
128 devices in a mesh: group: 8 (over y, core), member: 16 (over z, x).
Axes of the slice: x: 4, y: 4, z: 4, core: 2. Of those that a mesh axis runs over, the one named last changes fastest.
Arguments:
- hot_table: float32 [32768, 128], P('member'), may hold values from -6 to 6
- hot_acc: float32 [32768], P('member'), may hold values from 0.05 to 0.5
- cold_table: float32 [524288, 128], P(('group', 'member')), may hold values from -6 to 6
- cold_acc: float32 [524288], P(('group', 'member')), may hold values from 0.05 to 0.5
- bottom_out: bfloat16 [16384, 128], P(('group', 'member')), may hold values from -6 to 6
- labels: float32 [16384], P(('group', 'member')), may hold values from 0 to 1
- hot_owner: int32 [16384, 8, 2], P(('group', 'member')), may hold values from 0 to 15, all different within a row; in each aligned block of 1024 rows (0 to 1023, 1024 to 2047, ..., all dimensions but the last counted through in order) at most 256 rows name the same one
- hot_offset: int32 [16384, 8, 2], P(('group', 'member')), may hold values from 0 to 2047
- cold_owner: int32 [16384, 8, 1], P(('group', 'member')), may hold values from 0 to 127; in each aligned block of 1024 rows (0 to 1023, 1024 to 2047, ..., all dimensions but the last counted through in order) at most 32 rows name the same one
- cold_offset: int32 [16384, 8, 1], P(('group', 'member')), may hold values from 0 to 4095
- w_first: bfloat16 [1152, 2048], replicated, may hold values from -0.25 to 0.25
- w_second: bfloat16 [2048, 2048], replicated, may hold values from -0.1875 to 0.1875
- w_out: bfloat16 [2048], replicated, may hold values from -0.25 to 0.25
Outputs:
- new_hot: float32 [32768, 128], P('member')
- new_hot_acc: float32 [32768], P('member')
- new_cold: float32 [524288, 128], P(('group', 'member'))
- new_cold_acc: float32 [524288], P(('group', 'member'))
Inputs may be any that keep to these rules, and one draw needn't show every extreme that they name: `hot_owner`: the 2 entries of one sample and table differ. Among the 1024 sample-table pairs of one device, no member is named by more than 256 pairs, a bound that some block reaches. `cold_owner`: devices are numbered along group+member. Among the 1024 sample-table pairs of one device, no device is named by more than 32 pairs, and some device by exactly 32.
All inputs are finite; a program needn't handle non-finite values.
Results may differ from a plain program's by a relative error of at most 0.012.
Values may be sent and summed in bfloat16 or wider, within the bound.
A program may use at most 128 MiB of HBM per device.

v0:
```python
import jax
import jax.numpy as jnp
from jax import lax
from jax.sharding import PartitionSpec as P

STEP_RATE = 0.5


def place(owner_ids, offsets, owner_count, capacity):
    flat_owner = owner_ids.reshape(-1)
    flat_offset = offsets.reshape(-1)
    items = flat_owner.shape[0]
    owner_hits = (flat_owner[:, None] == jnp.arange(owner_count, dtype=jnp.int32)[None, :]).astype(
        jnp.bfloat16
    )
    order = jnp.arange(items, dtype=jnp.int32)
    earlier = (order[None, :] < order[:, None]).astype(jnp.bfloat16)
    before = jnp.dot(earlier, owner_hits, preferred_element_type=jnp.float32)
    slot_index = jnp.sum(before * owner_hits.astype(jnp.float32), axis=1).astype(jnp.int32)
    position = flat_owner * capacity + slot_index
    slot_onehot = (
        position[:, None] == jnp.arange(owner_count * capacity, dtype=jnp.int32)[None, :]
    ).astype(jnp.bfloat16)
    shifted = flat_offset + 1
    digits = jnp.stack([shifted // 64, shifted % 64], axis=1).astype(jnp.bfloat16)
    placed = jnp.einsum("ip,ic->pc", slot_onehot, digits, preferred_element_type=jnp.float32)
    requests = (placed[:, 0] * 64.0 + placed[:, 1]).astype(jnp.int32) - 1
    return (slot_onehot, requests.reshape(owner_count, capacity))


def serve(embedding, asked_rows):
    row_count, row_width = embedding.shape
    width = min(512, row_count)
    flat = asked_rows.reshape(-1)
    table_low = embedding.astype(jnp.bfloat16)

    def add_block(step, total):
        first = step * width
        columns = first + jnp.arange(width, dtype=jnp.int32)
        selector = (flat[:, None] == columns[None, :]).astype(jnp.bfloat16)
        rows = lax.dynamic_slice_in_dim(table_low, first, width, 0)
        return total + jnp.dot(selector, rows, preferred_element_type=jnp.float32)

    picked = lax.fori_loop(
        0, row_count // width, add_block, jnp.zeros((flat.shape[0], row_width), jnp.float32)
    )
    return picked.astype(jnp.bfloat16).reshape(asked_rows.shape + (row_width,))


def settle(embedding, asked_rows, received):
    row_count, row_width = embedding.shape
    width = min(512, row_count)
    flat = asked_rows.reshape(-1)
    values = received.reshape(flat.shape[0], row_width)

    def fill_block(step, total):
        first = step * width
        columns = first + jnp.arange(width, dtype=jnp.int32)
        selector = (flat[:, None] == columns[None, :]).astype(jnp.float32)
        block_sum = jnp.einsum(
            "sr,se->re",
            selector,
            values,
            precision=lax.Precision.HIGHEST,
            preferred_element_type=jnp.float32,
        )
        return lax.dynamic_update_slice_in_dim(total, block_sum, first, 0)

    return lax.fori_loop(
        0, row_count // width, fill_block, jnp.zeros((row_count, row_width), jnp.float32)
    )


def spread(slot_onehot, terms):
    return jnp.einsum(
        "ip,ie->pe",
        slot_onehot.astype(jnp.float32),
        terms,
        precision=lax.Precision.HIGHEST,
        preferred_element_type=jnp.float32,
    )


def update(embedding, accum, gradient):
    new_accum = accum + jnp.mean(gradient * gradient, axis=1)
    return (embedding - STEP_RATE * gradient / jnp.sqrt(new_accum)[:, None], new_accum)


def shards(
    hot_table,
    hot_acc,
    cold_table,
    cold_acc,
    bottom_out,
    labels,
    hot_owner,
    hot_offset,
    cold_owner,
    cold_offset,
    w_first,
    w_second,
    w_out,
):
    members = lax.axis_size("member")
    groups = lax.axis_size("group")
    devices = members * groups
    samples, tables, hot_per = hot_owner.shape
    cold_per = cold_owner.shape[2]
    row_width = hot_table.shape[1]
    hot_cap = 2 * samples * tables * hot_per // members
    cold_cap = 4 * samples * tables * cold_per // devices
    hot_onehot, hot_requests = place(hot_owner, hot_offset, members, hot_cap)
    asked_rows = lax.all_to_all(hot_requests, "member", split_axis=0, concat_axis=0, tiled=True)
    hot_back = lax.all_to_all(
        serve(hot_table, asked_rows), "member", split_axis=0, concat_axis=0, tiled=True
    )
    hot_asked = asked_rows
    hot_vals = jnp.dot(
        hot_onehot, hot_back.reshape(-1, row_width), preferred_element_type=jnp.float32
    )
    hot_vals = hot_vals.reshape(samples, tables, hot_per, row_width)
    cold_onehot, cold_requests = place(cold_owner, cold_offset, devices, cold_cap)
    asked_rows = lax.all_to_all(
        cold_requests, ("group", "member"), split_axis=0, concat_axis=0, tiled=True
    )
    cold_back = lax.all_to_all(
        serve(cold_table, asked_rows), ("group", "member"), split_axis=0, concat_axis=0, tiled=True
    )
    cold_vals = jnp.dot(
        cold_onehot, cold_back.reshape(-1, row_width), preferred_element_type=jnp.float32
    )
    cold_vals = cold_vals.reshape(samples, tables, cold_per, row_width)
    pooled = (jnp.sum(hot_vals, axis=2) + jnp.sum(cold_vals, axis=2)).astype(jnp.bfloat16)
    features = jnp.concatenate([bottom_out, pooled.reshape(samples, tables * row_width)], axis=1)
    first_pre = jnp.dot(features, w_first, preferred_element_type=jnp.float32)
    first_act = jnp.maximum(first_pre, 0.0).astype(jnp.bfloat16)
    second_pre = jnp.dot(first_act, w_second, preferred_element_type=jnp.float32)
    second_act = jnp.maximum(second_pre, 0.0).astype(jnp.bfloat16)
    score = jnp.dot(second_act, w_out, preferred_element_type=jnp.float32)
    delta = jax.nn.sigmoid(score) - labels
    grad_second = jnp.where(
        second_pre > 0, delta[:, None] * w_out.astype(jnp.float32)[None, :], 0.0
    ).astype(jnp.bfloat16)
    back_second = jnp.einsum("bk,hk->bh", grad_second, w_second, preferred_element_type=jnp.float32)
    grad_first = jnp.where(first_pre > 0, back_second, 0.0).astype(jnp.bfloat16)
    grad_features = jnp.einsum("bk,hk->bh", grad_first, w_first, preferred_element_type=jnp.float32)
    grad_pooled = grad_features[:, row_width:].reshape(samples, tables, 1, row_width)
    hot_terms = jnp.broadcast_to(grad_pooled, (samples, tables, hot_per, row_width)).reshape(
        -1, row_width
    )
    hot_send = spread(hot_onehot, hot_terms).reshape(members, hot_cap, row_width)
    hot_recv = lax.all_to_all(hot_send, "member", split_axis=0, concat_axis=0, tiled=True)
    hot_local = settle(hot_table, hot_asked, hot_recv)
    hot_grad = lax.psum(hot_local, "group")
    cold_terms = grad_pooled.reshape(-1, row_width)
    cold_send = spread(cold_onehot, cold_terms).reshape(devices, cold_cap, row_width)
    cold_recv = lax.all_to_all(
        cold_send.astype(jnp.bfloat16), ("group", "member"), split_axis=0, concat_axis=0, tiled=True
    ).astype(cold_send.dtype)
    cold_grad = settle(cold_table, asked_rows, cold_recv)
    new_hot, new_hot_acc = update(hot_table, hot_acc, hot_grad)
    new_cold, new_cold_acc = update(cold_table, cold_acc, cold_grad)
    return (new_hot, new_hot_acc, new_cold, new_cold_acc)


def solution(mesh):
    in_specs = (
        P("member", None),
        P("member"),
        P(("group", "member"), None),
        P(("group", "member")),
        P(("group", "member"), None),
        P(("group", "member")),
        P(("group", "member"), None, None),
        P(("group", "member"), None, None),
        P(("group", "member"), None, None),
        P(("group", "member"), None, None),
        P(),
        P(),
        P(),
    )
    out_specs = (
        P("member", None),
        P("member"),
        P(("group", "member"), None),
        P(("group", "member")),
    )
    return jax.shard_map(shards, mesh=mesh, in_specs=in_specs, out_specs=out_specs, check_vma=False)
```

profile of v0, /device:TPU:0, one launch (start us, length us, event | category | flops | bytes accessed | tf_op | source)
XLA Modules:
  0.0 373.6 jit_solution(9977785380953094563)
XLA Ops:
  10.6 5.8 %fusion.37 = f32[4096,2]{0,1:T(2,128)S(1)} fusion(s32[2048]{0:T(1024)S(1)} %multiply_add_fusion.4, bf16[2048,1]{0,1:T(2,128)(2,1)S(1)} %fusion.100, bf16[2048,1]{0,1:T(2,128)(2,1)S(1)} %get-tuple-element.392), kind=kOutput, calls=%fused_computation.34 | convolution fusion | flops 41959424 | bytes 49152 | tf_op jit(solution)/shard_map/ip,ic->pc/dot_general | solution.py:26
  17.1 8.4 %all-to-all-start = ((s32[16,1,256]{2,1,0:T(1,128)}), s32[16,1,256]{2,1,0:T(1,128)S(1)}, u32[]{:S(2)}, u32[]{:S(2)}) async-start(s32[16,1,256]{2,1,0:T(1,128)} %bitcast), calls=%async_computation | async-start | bytes 32768 | tf_op jit(solution)/shard_map/all_to_all | solution.py:113
  34.9 10.5 %all-to-all-start.2 = ((s32[128,1,32]{2,1,0:T(1,128)}), s32[128,1,32]{2,1,0:T(1,128)S(1)}, u32[]{:S(2)}, u32[]{:S(2)}) async-start(s32[128,1,32]{2,1,0:T(1,128)} %bitcast.8), calls=%async_computation.2 | async-start | bytes 131072 | tf_op jit(solution)/shard_map/all_to_all | solution.py:123
  45.4 12.9 %while.57 = (s32[]{:T(128)}, f32[4096,128]{1,0:T(8,128)S(1)}, s32[16,256]{1,0:T(8,128)S(1)}, bf16[2048,128]{1,0:T(8,128)(2,1)}, s32[]{:T(128)}, /*index=5*/s32[]{:T(128)}, s32[]{:T(128)}, s32[]{:T(128)}) while((s32[]{:T(128)}, f32[4096,128]{1,0:T(8,128)S(1)}, s32[16,256]{1,0:T(8,128)S(1)}, bf16[2048,128]{1,0:T(8,128)(2,1)}, ...), condition=%wide.region_2.3_spmd.clone, body=%wide.region_1.2_spmd.clone.sunk | while | flops 540017152 | bytes 4378773 | solution.py:44
  62.4 6.7 %all-to-all-start.1 = ((bf16[16,256,128]{2,1,0:T(8,128)(2,1)}), bf16[16,256,128]{2,1,0:T(8,128)(2,1)}, u32[]{:S(2)}, u32[]{:S(2)}) async-start(bf16[16,256,128]{2,1,0:T(8,128)(2,1)} %bitcast.2), calls=%async_computation.1 | async-start | bytes 2097152 | tf_op jit(solution)/shard_map/all_to_all | solution.py:114
  69.3 25.6 %while.59 = (s32[]{:T(128)}, f32[4096,128]{1,0:T(8,128)S(1)}, s32[128,32]{1,0:T(8,128)}, bf16[4096,128]{1,0:T(8,128)(2,1)}, s32[4096]{0:T(1024)S(1)}, /*index=5*/s32[]{:T(128)}, s32[]{:T(128)}, s32[]{:T(128)}, s32[]{:T(128)}) while((s32[]{:T(128)}, f32[4096,128]{1,0:T(8,128)S(1)}, s32[128,32]{1,0:T(8,128)}, ...), condition=%wide.wide.region_6.7_spmd.clone, body=%wide.wide.region_5.6_spmd.clone.sunk | while | flops 540017152 | bytes 4346013 | solution.py:44
  95.9 10.4 %all-to-all-start.3 = ((bf16[128,32,128]{2,1,0:T(8,128)(2,1)}), bf16[128,32,128]{2,1,0:T(8,128)(2,1)S(1)}, u32[]{:S(2)}, u32[]{:S(2)}) async-start(bf16[128,32,128]{2,1,0:T(8,128)(2,1)} %bitcast.10), calls=%async_computation.3 | async-start | bytes 2097152 | tf_op jit(solution)/shard_map/all_to_all | solution.py:126
  106.7 7.3 %fusion.61 = f32[128,8,128]{2,0,1:T(8,128)S(1)} fusion(bf16[4096,128,1,1]{1,0,3,2:T(8,128)(2,1)} %bitcast.5, s32[128,8,2]{0,2,1:T(2,128)S(1)} %copy.51), kind=kOutput, calls=%fused_computation.62 | convolution fusion | flops 2156003328 | bytes 1581056 | tf_op jit(solution)/shard_map/dot_general | solution.py:118
  114.2 11.0 %all-to-all-done.3 = bf16[128,32,128]{2,1,0:T(8,128)(2,1)S(1)} async-done(((bf16[128,32,128]{2,1,0:T(8,128)(2,1)}), bf16[128,32,128]{2,1,0:T(8,128)(2,1)S(1)}, u32[]{:S(2)}, u32[]{:S(2)}) %all-to-all-start.3) | async-done | bytes 1048608 | tf_op jit(solution)/shard_map/all_to_all | solution.py:126
  125.2 3.5 fusion.68
  128.8 3.2 fusion.88
  132.0 4.9 %fusion.78 = f32[128,2048]{1,0:T(8,128)S(1)} fusion(bf16[2048,2048]{1,0:T(8,128)(2,1)} %param.32, f32[128,2048]{1,0:T(8,128)S(1)} %fusion.88), kind=kOutput, calls=%fused_computation.80 | convolution fusion | flops 1074266112 | bytes 10485760 | tf_op jit(solution)/shard_map/dot_general | solution.py:137
  137.1 9.7 %fusion.53 = f32[128,1024]{1,0:T(8,128)} fusion(bf16[1152,2048]{1,0:T(8,128)(2,1)} %param.31, bf16[2048,2048]{1,0:T(8,128)(2,1)} %param.32, f32[128,2048]{1,0:T(8,128)S(1)} %fusion.88, f32[128,2048]{1,0:T(8,128)S(1)} %fusion.78, f32[2048]{0:T(1024)S(1)} %convert_element_type.134, f32[128]{0:T(128)S(1)} %fusion.77), kind=kOutput, calls=%fused_computation.52 | convolution fusion | flops 1612447744 | bytes 15213056 | tf_op jit(solution)/shard_map/bk,hk->bh/dot_general | solution.py:146
  148.0 6.9 %fusion.58 = bf16[128,32,128]{2,0,1:T(8,128)(2,1)S(1)} fusion(f32[1024,128,1]{1,0,2:T(8,128)S(1)} %reshape.436, s32[128,32]{0,1:T(8,128)S(1)} %multiply_add_fusion.1, s32[1024]{0:T(1024)S(1)} %multiply_add_fusion.5), kind=kOutput, calls=%fused_computation.61 | convolution fusion | flops 6447169536 | bytes 1593344 | tf_op jit(solution)/shard_map/ip,ie->pe/dot_general | solution.py:75
  156.6 5.0 %all-to-all-start.5 = ((bf16[128,32,128]{2,1,0:T(8,128)(2,1)}), bf16[128,32,128]{2,1,0:T(8,128)(2,1)S(1)}, u32[]{:S(2)}, u32[]{:S(2)}) async-start(bf16[128,32,128]{2,1,0:T(8,128)(2,1)} %copy.60), calls=%async_computation.5 | async-start | bytes 2097152 | tf_op jit(solution)/shard_map/all_to_all | solution.py:157
  162.2 15.3 %fusion.33 = f32[16,256,128]{2,1,0:T(8,128)} fusion(f32[2048,128,1]{1,0,2:T(8,128)S(1)} %bitcast.88, s32[16,256]{1,0:T(8,128)S(1)} %multiply_add_fusion.2, s32[2048]{0:T(1024)S(1)} %multiply_add_fusion.4), kind=kOutput, calls=%fused_computation.31 | convolution fusion | flops 12893290496 | bytes 3170304 | tf_op jit(solution)/shard_map/ip,ie->pe/dot_general | solution.py:75
  180.3 4.4 %all-to-all-start.4 = ((f32[16,256,128]{2,1,0:T(8,128)}), f32[16,256,128]{2,1,0:T(8,128)}, u32[]{:S(2)}, u32[]{:S(2)}) async-start(f32[16,256,128]{2,1,0:T(8,128)} %fusion.33), calls=%async_computation.4 | async-start | bytes 4194304 | tf_op jit(solution)/shard_map/all_to_all | solution.py:152
  186.4 70.9 %while.58 = (s32[]{:T(128)}, f32[4096,128]{1,0:T(8,128)S(1)}, s32[128,32]{1,0:T(8,128)}, f32[4096,128]{1,0:T(8,128)}, s32[4096]{0:T(1024)S(1)}, /*index=5*/s32[]{:T(128)}, s32[]{:T(128)}, s32[]{:T(128)}, s32[]{:T(128)}) while((s32[]{:T(128)}, f32[4096,128]{1,0:T(8,128)S(1)}, s32[128,32]{1,0:T(8,128)}, f32[4096,128]{1,0:T(8,128)}, ...), condition=%wide.wide.region_12.13_spmd, body=%wide.wide.region_11.12_spmd.sunk | while | flops 3223323136 | bytes 2379923 | solution.py:69
  186.5 8.8 %fusion.156 = f32[4096,128]{1,0:T(8,128)S(1)} fusion(f32[4096,128]{1,0:T(8,128)S(1)} %get-tuple-element.623, s32[]{:T(128)S(6)} %select_n.122, f32[4096,128]{1,0:T(8,128)} %get-tuple-element.634, s32[512]{0:T(512)S(1)} %iota_add_fusion.12, s32[4096]{0:T(1024)S(1)} %get-tuple-element.635), kind=kOutput, calls=%fused_computation.10.clone.clone.1 | convolution fusion | flops 3223322624 | bytes 2377732 | tf_op jit(solution)/shard_map/while/body/eval_jaxpr/sr,se->re/dot_general | solution.py:60
  195.3 8.8 %fusion.156 = f32[4096,128]{1,0:T(8,128)S(1)} fusion(f32[4096,128]{1,0:T(8,128)S(1)} %get-tuple-element.623, s32[]{:T(128)S(6)} %select_n.122, f32[4096,128]{1,0:T(8,128)} %get-tuple-element.634, s32[512]{0:T(512)S(1)} %iota_add_fusion.12, s32[4096]{0:T(1024)S(1)} %get-tuple-element.635), kind=kOutput, calls=%fused_computation.10.clone.clone.1 | convolution fusion | flops 3223322624 | bytes 2377732 | tf_op jit(solution)/shard_map/while/body/eval_jaxpr/sr,se->re/dot_general | solution.py:60
  204.2 8.8 %fusion.156 = f32[4096,128]{1,0:T(8,128)S(1)} fusion(f32[4096,128]{1,0:T(8,128)S(1)} %get-tuple-element.623, s32[]{:T(128)S(6)} %select_n.122, f32[4096,128]{1,0:T(8,128)} %get-tuple-element.634, s32[512]{0:T(512)S(1)} %iota_add_fusion.12, s32[4096]{0:T(1024)S(1)} %get-tuple-element.635), kind=kOutput, calls=%fused_computation.10.clone.clone.1 | convolution fusion | flops 3223322624 | bytes 2377732 | tf_op jit(solution)/shard_map/while/body/eval_jaxpr/sr,se->re/dot_general | solution.py:60
  213.0 8.8 %fusion.156 = f32[4096,128]{1,0:T(8,128)S(1)} fusion(f32[4096,128]{1,0:T(8,128)S(1)} %get-tuple-element.623, s32[]{:T(128)S(6)} %select_n.122, f32[4096,128]{1,0:T(8,128)} %get-tuple-element.634, s32[512]{0:T(512)S(1)} %iota_add_fusion.12, s32[4096]{0:T(1024)S(1)} %get-tuple-element.635), kind=kOutput, calls=%fused_computation.10.clone.clone.1 | convolution fusion | flops 3223322624 | bytes 2377732 | tf_op jit(solution)/shard_map/while/body/eval_jaxpr/sr,se->re/dot_general | solution.py:60
  221.9 8.8 %fusion.156 = f32[4096,128]{1,0:T(8,128)S(1)} fusion(f32[4096,128]{1,0:T(8,128)S(1)} %get-tuple-element.623, s32[]{:T(128)S(6)} %select_n.122, f32[4096,128]{1,0:T(8,128)} %get-tuple-element.634, s32[512]{0:T(512)S(1)} %iota_add_fusion.12, s32[4096]{0:T(1024)S(1)} %get-tuple-element.635), kind=kOutput, calls=%fused_computation.10.clone.clone.1 | convolution fusion | flops 3223322624 | bytes 2377732 | tf_op jit(solution)/shard_map/while/body/eval_jaxpr/sr,se->re/dot_general | solution.py:60
  230.7 8.8 %fusion.156 = f32[4096,128]{1,0:T(8,128)S(1)} fusion(f32[4096,128]{1,0:T(8,128)S(1)} %get-tuple-element.623, s32[]{:T(128)S(6)} %select_n.122, f32[4096,128]{1,0:T(8,128)} %get-tuple-element.634, s32[512]{0:T(512)S(1)} %iota_add_fusion.12, s32[4096]{0:T(1024)S(1)} %get-tuple-element.635), kind=kOutput, calls=%fused_computation.10.clone.clone.1 | convolution fusion | flops 3223322624 | bytes 2377732 | tf_op jit(solution)/shard_map/while/body/eval_jaxpr/sr,se->re/dot_general | solution.py:60
  239.6 8.8 %fusion.156 = f32[4096,128]{1,0:T(8,128)S(1)} fusion(f32[4096,128]{1,0:T(8,128)S(1)} %get-tuple-element.623, s32[]{:T(128)S(6)} %select_n.122, f32[4096,128]{1,0:T(8,128)} %get-tuple-element.634, s32[512]{0:T(512)S(1)} %iota_add_fusion.12, s32[4096]{0:T(1024)S(1)} %get-tuple-element.635), kind=kOutput, calls=%fused_computation.10.clone.clone.1 | convolution fusion | flops 3223322624 | bytes 2377732 | tf_op jit(solution)/shard_map/while/body/eval_jaxpr/sr,se->re/dot_general | solution.py:60
  248.5 8.8 %fusion.156 = f32[4096,128]{1,0:T(8,128)S(1)} fusion(f32[4096,128]{1,0:T(8,128)S(1)} %get-tuple-element.623, s32[]{:T(128)S(6)} %select_n.122, f32[4096,128]{1,0:T(8,128)} %get-tuple-element.634, s32[512]{0:T(512)S(1)} %iota_add_fusion.12, s32[4096]{0:T(1024)S(1)} %get-tuple-element.635), kind=kOutput, calls=%fused_computation.10.clone.clone.1 | convolution fusion | flops 3223322624 | bytes 2377732 | tf_op jit(solution)/shard_map/while/body/eval_jaxpr/sr,se->re/dot_general | solution.py:60
  259.7 38.4 %while.56 = (s32[]{:T(128)}, f32[2048,128]{1,0:T(8,128)}, s32[16,256]{1,0:T(8,128)S(1)}, f32[4096,128]{1,0:T(8,128)}, s32[]{:T(128)}, /*index=5*/s32[]{:T(128)}, s32[]{:T(128)}, s32[]{:T(128)}) while((s32[]{:T(128)}, f32[2048,128]{1,0:T(8,128)}, s32[16,256]{1,0:T(8,128)S(1)}, f32[4096,128]{1,0:T(8,128)}, s32[]{:T(128)}, /*index=5*/s32[]{:T(128)}, ...), condition=%wide.region_8.9_spmd, body=%wide.region_7.8_spmd.sunk | while | flops 3223323136 | bytes 2412683 | solution.py:69
  259.9 9.5 %fusion.150 = f32[2048,128]{1,0:T(8,128)} fusion(f32[2048,128]{1,0:T(8,128)} %get-tuple-element.598, s32[]{:T(128)S(6)} %select_n.120, f32[4096,128]{1,0:T(8,128)} %get-tuple-element.608, s32[512]{0:T(512)S(1)} %iota_add_fusion.10, s32[4096]{0:T(1024)S(1)} %bitcast.93), kind=kOutput, calls=%fused_computation.4.clone.1 | convolution fusion | flops 3223322624 | bytes 2377732 | tf_op jit(solution)/shard_map/while/body/eval_jaxpr/sr,se->re/dot_general | solution.py:60
  269.5 9.5 %fusion.150 = f32[2048,128]{1,0:T(8,128)} fusion(f32[2048,128]{1,0:T(8,128)} %get-tuple-element.598, s32[]{:T(128)S(6)} %select_n.120, f32[4096,128]{1,0:T(8,128)} %get-tuple-element.608, s32[512]{0:T(512)S(1)} %iota_add_fusion.10, s32[4096]{0:T(1024)S(1)} %bitcast.93), kind=kOutput, calls=%fused_computation.4.clone.1 | convolution fusion | flops 3223322624 | bytes 2377732 | tf_op jit(solution)/shard_map/while/body/eval_jaxpr/sr,se->re/dot_general | solution.py:60
  279.0 9.5 %fusion.150 = f32[2048,128]{1,0:T(8,128)} fusion(f32[2048,128]{1,0:T(8,128)} %get-tuple-element.598, s32[]{:T(128)S(6)} %select_n.120, f32[4096,128]{1,0:T(8,128)} %get-tuple-element.608, s32[512]{0:T(512)S(1)} %iota_add_fusion.10, s32[4096]{0:T(1024)S(1)} %bitcast.93), kind=kOutput, calls=%fused_computation.4.clone.1 | convolution fusion | flops 3223322624 | bytes 2377732 | tf_op jit(solution)/shard_map/while/body/eval_jaxpr/sr,se->re/dot_general | solution.py:60
  288.5 9.5 %fusion.150 = f32[2048,128]{1,0:T(8,128)} fusion(f32[2048,128]{1,0:T(8,128)} %get-tuple-element.598, s32[]{:T(128)S(6)} %select_n.120, f32[4096,128]{1,0:T(8,128)} %get-tuple-element.608, s32[512]{0:T(512)S(1)} %iota_add_fusion.10, s32[4096]{0:T(1024)S(1)} %bitcast.93), kind=kOutput, calls=%fused_computation.4.clone.1 | convolution fusion | flops 3223322624 | bytes 2377732 | tf_op jit(solution)/shard_map/while/body/eval_jaxpr/sr,se->re/dot_general | solution.py:60
  301.0 60.7 %all-reduce.2.cloned.1.call-done = f32[2048,128]{1,0:T(8,128)} async-done(((f32[2048,128]{1,0:T(8,128)}), f32[2048,128]{1,0:T(8,128)}) %all-reduce.2.cloned.1.call-update) | async-done | bytes 1048592 | tf_op jit(solution)/shard_map/psum | solution.py:154
  (145 shorter events, 75.0 us)
Async XLA Ops:
  8.4 1.5 copy-start.12
  10.6 14.9 %copy-start.14 = (s32[128,8,1]{0,2,1:T(1,128)S(1)}, s32[128,8,1]{0,2,1:T(1,128)}, u32[]{:S(2)}) copy-start(s32[128,8,1]{0,2,1:T(1,128)} %param.29) | copy-start | bytes 12292
  16.5 9.9 %copy-start.15 = (s32[128,8,1]{0,2,1:T(1,128)S(1)}, s32[128,8,1]{0,2,1:T(1,128)}, u32[]{:S(2)}) copy-start(s32[128,8,1]{0,2,1:T(1,128)} %param.30) | copy-start | bytes 12292
  17.1 17.8 %all-to-all-start = ((s32[16,1,256]{2,1,0:T(1,128)}), s32[16,1,256]{2,1,0:T(1,128)S(1)}, u32[]{:S(2)}, u32[]{:S(2)}) async-start(s32[16,1,256]{2,1,0:T(1,128)} %bitcast), calls=%async_computation | async-start | bytes 32768 | tf_op jit(solution)/shard_map/all_to_all | solution.py:113
  26.7 3.1 copy-start.10
  26.7 3.8 %copy-start = (f32[4096,128]{1,0:T(8,128)S(1)}, f32[4096,128]{1,0:T(8,128)}, u32[]{:S(2)}) copy-start(f32[4096,128]{1,0:T(8,128)} %param.23) | copy-start | bytes 6291460
  29.6 1.9 copy-start.1
  31.6 13.9 %copy-start.3 = (f32[4096,128]{1,0:T(8,128)S(1)}, f32[4096,128]{1,0:T(8,128)}, u32[]{:S(2)}) copy-start(f32[4096,128]{1,0:T(8,128)} %custom-call) | copy-start | bytes 6291460
  34.9 27.5 %all-to-all-start.2 = ((s32[128,1,32]{2,1,0:T(1,128)}), s32[128,1,32]{2,1,0:T(1,128)S(1)}, u32[]{:S(2)}, u32[]{:S(2)}) async-start(s32[128,1,32]{2,1,0:T(1,128)} %bitcast.8), calls=%async_computation.2 | async-start | bytes 131072 | tf_op jit(solution)/shard_map/all_to_all | solution.py:123
  58.3 1.3 copy-start.4
  59.6 9.6 %copy-start.2 = (f32[4096,128]{1,0:T(8,128)S(1)}, f32[4096,128]{1,0:T(8,128)}, u32[]{:S(2)}) copy-start(f32[4096,128]{1,0:T(8,128)} %custom-call.1) | copy-start | bytes 6291460
  62.4 6.8 %copy-start.6 = (s32[128,1,32]{2,1,0:T(1,128)}, s32[128,1,32]{2,1,0:T(1,128)S(1)}, u32[]{:S(2)}) copy-start(s32[128,1,32]{2,1,0:T(1,128)S(1)} %all-to-all-done.2) | copy-start | bytes 49156
  62.4 33.5 %all-to-all-start.1 = ((bf16[16,256,128]{2,1,0:T(8,128)(2,1)}), bf16[16,256,128]{2,1,0:T(8,128)(2,1)}, u32[]{:S(2)}, u32[]{:S(2)}) async-start(bf16[16,256,128]{2,1,0:T(8,128)(2,1)} %bitcast.2), calls=%async_computation.1 | async-start | bytes 2097152 | tf_op jit(solution)/shard_map/all_to_all | solution.py:114
  94.8 11.5 %copy-start.8 = (s32[128,8,2]{0,2,1:T(2,128)S(1)}, s32[128,8,2]{0,2,1:T(2,128)}, u32[]{:S(2)}) copy-start(s32[128,8,2]{0,2,1:T(2,128)} %param.27) | copy-start | bytes 24580
  94.8 11.7 %copy-start.9 = (bf16[128,128]{1,0:T(8,128)(2,1)S(1)}, bf16[128,128]{1,0:T(8,128)(2,1)}, u32[]{:S(2)}) copy-start(bf16[128,128]{1,0:T(8,128)(2,1)} %param.25) | copy-start | bytes 98308
  95.9 29.3 %all-to-all-start.3 = ((bf16[128,32,128]{2,1,0:T(8,128)(2,1)}), bf16[128,32,128]{2,1,0:T(8,128)(2,1)S(1)}, u32[]{:S(2)}, u32[]{:S(2)}) async-start(bf16[128,32,128]{2,1,0:T(8,128)(2,1)} %bitcast.10), calls=%async_computation.3 | async-start | bytes 2097152 | tf_op jit(solution)/shard_map/all_to_all | solution.py:126
  132.0 4.9 %copy-start.16 = (f32[128]{0:T(128)S(1)}, f32[128]{0:T(128)}, u32[]{:S(2)}) copy-start(f32[128]{0:T(128)} %param.26) | copy-start | bytes 1540
  154.9 6.7 %copy-start.7 = (s32[128,32]{1,0:T(8,128)S(1)}, s32[128,32]{1,0:T(8,128)}, u32[]{:S(2)}) copy-start(s32[128,32]{1,0:T(8,128)} %get-tuple-element.650) | copy-start | bytes 49156
  154.9 6.8 %copy-start.5 = (f32[128,1024]{1,0:T(8,128)S(1)}, f32[128,1024]{1,0:T(8,128)}, u32[]{:S(2)}) copy-start(f32[128,1024]{1,0:T(8,128)} %fusion.53) | copy-start | bytes 1572868
  156.6 23.7 %all-to-all-start.5 = ((bf16[128,32,128]{2,1,0:T(8,128)(2,1)}), bf16[128,32,128]{2,1,0:T(8,128)(2,1)S(1)}, u32[]{:S(2)}, u32[]{:S(2)}) async-start(bf16[128,32,128]{2,1,0:T(8,128)(2,1)} %copy.60), calls=%async_computation.5 | async-start | bytes 2097152 | tf_op jit(solution)/shard_map/all_to_all | solution.py:157
  180.3 78.4 %all-to-all-start.4 = ((f32[16,256,128]{2,1,0:T(8,128)}), f32[16,256,128]{2,1,0:T(8,128)}, u32[]{:S(2)}, u32[]{:S(2)}) async-start(f32[16,256,128]{2,1,0:T(8,128)} %fusion.33), calls=%async_computation.4 | async-start | bytes 4194304 | tf_op jit(solution)/shard_map/all_to_all | solution.py:152
  184.7 177.1 %all-reduce.2.cloned.1.call-start = ((), (), s32[]{:S(2)}) async-start(), calls=%async_computation.6 | async-start | bytes 2097152 | tf_op jit(solution)/shard_map/psum | solution.py:154
  257.3 0.7 copy-start.11
  298.1 65.2 %copy-start.13 = (f32[2048]{0:T(1024)S(1)}, f32[2048]{0:T(1024)}, u32[]{:S(2)}) copy-start(f32[2048]{0:T(1024)} %param.22) | copy-start | bytes 24580
Sparse Core Ops, SparseCore 0:
  298.2 63.5 all-reduce.1
where the time goes:
time: 381 us; the launch traced here: 374 us
  matrix products  209 us (55%)
  waiting for transfers between devices  74.5 us (20%)
  starting transfers between devices  45.6 us (12%)
  other arithmetic  17.1 us (4%)
  between operations  14.8 us (4%)
  local copies, waits for them, and re-layouts  12 us (3%)
    dot_general x12, matrix products, fill_block(): jnp.einsum('sr,se->re', selector, values, precision=lax.Precision.HIGHEST...  109 us
    psum x1, waiting for transfers between devices, shards(): hot_grad = lax.psum(hot_local, 'group')  60.7 us
    dot_general x12, matrix products, add_block(): return total + jnp.dot(selector, rows, preferred_element_type=jnp.float32)  37.8 us
    dot_general x2, matrix products, spread(): jnp.einsum('ip,ie->pe', slot_onehot.astype(jnp.float32), terms, precision...  22.3 us
    all_to_all x1, waiting for transfers between devices, shards(): lax.all_to_all(serve(cold_table, asked_rows), ('group', 'member'), split_...  11 us
    all_to_all x1, starting transfers between devices, shards(): lax.all_to_all(cold_requests, ('group', 'member'), split_axis=0, concat_a...  10.5 us
    all_to_all x1, starting transfers between devices, shards(): lax.all_to_all(serve(cold_table, asked_rows), ('group', 'member'), split_...  10.4 us
    dot_general x1, matrix products, shards(): jnp.einsum('bk,hk->bh', grad_first, w_first, preferred_element_type=jnp.f...  9.71 us
  transfers between devices with their start and end apart: 7, of which 3 were waited for; matrix products, arithmetic and copies ran while one was open for 40% of the time, Pallas kernels for 0%

commit v1 on v0

v1 whole, which is shorter than its diff:
```python
import functools
import jax
import jax.numpy as jnp
from jax import lax
from jax.experimental import pallas as pl
from jax.experimental.pallas import tpu as pltpu
from jax.sharding import PartitionSpec as P
V = pl.BlockSpec(memory_space=pltpu.VMEM)
S = pl.BlockSpec(memory_space=pltpu.SMEM)
BIG = pltpu.CompilerParams(vmem_limit_bytes=56 << 20)

def place_one(owner_ref, offset_ref, n, cap, req_ref, pos_ref):
    R = owner_ref.shape[0]
    own = lax.broadcasted_iota(jnp.int32, (n, 128), 0)
    masks = [(owner_ref[r:r + 1, :] == own) for r in range(R)]
    low = [m.astype(jnp.float32) for m in masks]
    stacked = jnp.concatenate(low, axis=0).astype(jnp.bfloat16)
    a = lax.broadcasted_iota(jnp.int32, (128, 128), 0)
    b = lax.broadcasted_iota(jnp.int32, (128, 128), 1)
    tri = (a < b).astype(jnp.float32)
    side = jnp.concatenate([tri, jnp.ones((128, 128), jnp.float32)], axis=1).astype(jnp.bfloat16)
    counts = jnp.dot(stacked, side, preferred_element_type=jnp.float32)
    base = jnp.zeros((n, 128), jnp.float32)
    his, los, hots = [], [], []
    capi = lax.broadcasted_iota(jnp.int32, (cap, 128), 0)
    for r in range(R):
        c = counts[r * n:(r + 1) * n]
        slot = jnp.sum(low[r] * (c[:, :128] + base), axis=0, keepdims=True).astype(jnp.int32)
        base = base + c[:, 128:]
        pos_ref[r:r + 1, :] = owner_ref[r:r + 1, :] * cap + slot
        off = offset_ref[r:r + 1, :]
        his.append(low[r] * (off // 64).astype(jnp.float32))
        los.append(low[r] * (off % 64).astype(jnp.float32))
        hots.append((capi == slot).astype(jnp.float32).astype(jnp.bfloat16))
    A = jnp.concatenate([jnp.concatenate(his, axis=1), jnp.concatenate(los, axis=1)], axis=0).astype(jnp.bfloat16)
    B = jnp.concatenate(hots, axis=1)
    got = lax.dot_general(A, B, (((1,), (1,)), ((), ())), preferred_element_type=jnp.float32)
    req_ref[...] = (got[:n] * 64.0 + got[n:]).astype(jnp.int32)

def place_kernel(ho, hf, co, cf, hreq, hpos, creq, cpos):
    place_one(ho, hf, 16, 256, hreq, hpos)
    place_one(co, cf, 128, 32, creq, cpos)

def place(ho, hf, co, cf):
    return pl.pallas_call(place_kernel, out_shape=[jax.ShapeDtypeStruct(s, jnp.int32) for s in [(16,256),(16,128),(128,32),(8,128)]],
        in_specs=[V]*4, out_specs=[V]*4, compiler_params=BIG, name="place")(ho, hf, co, cf)

def serve_kernel(U, CH, idx_ref, tab_ref, out_ref, stage):
    n = out_ref.shape[0]
    def chunk(c, _):
        base = c * CH
        for j in range(CH):
            stage[pl.ds(j, 1), :] = tab_ref[pl.ds(idx_ref[base + j], 1), :]
        out_ref[pl.ds(pl.multiple_of(base, CH), CH), :] = stage[...].astype(jnp.bfloat16)
        return 0
    lax.fori_loop(0, n // CH, chunk, 0)

def serve(idx, tab, CH=32, U=8):
    return pl.pallas_call(functools.partial(serve_kernel, U, CH), out_shape=jax.ShapeDtypeStruct((idx.shape[0],128), jnp.bfloat16),
        in_specs=[S, V], out_specs=V, scratch_shapes=[pltpu.VMEM((CH,128), jnp.float32)], compiler_params=BIG, name="serve")(idx, tab)

def settle_kernel(BR, BK, idx_ref, val_ref, out_ref):
    rows = out_ref.shape[0]
    K = val_ref.shape[0]
    def blk(i, _):
        first = i * BR
        it = lax.broadcasted_iota(jnp.int32, (BR, BK), 0)
        acc = jnp.zeros((BR, 128), jnp.float32)
        for k in range(K // BK):
            rel = idx_ref[:, k * BK:(k + 1) * BK] - first
            oh = jnp.where(it == rel, 1.0, 0.0).astype(jnp.bfloat16)
            acc = acc + jnp.dot(oh, val_ref[k * BK:(k + 1) * BK, :], preferred_element_type=jnp.float32)
        out_ref[pl.ds(pl.multiple_of(first, BR), BR), :] = acc
        return 0
    lax.fori_loop(0, rows // BR, blk, 0)

def settle(idx, val, rows, BR=256, BK=512):
    return pl.pallas_call(functools.partial(settle_kernel, BR, BK), out_shape=jax.ShapeDtypeStruct((rows,128), jnp.float32),
        in_specs=[V, V], out_specs=V, compiler_params=BIG, name="settle")(idx.reshape(1,-1), val)

def rmw_kernel(NB, CH, idx_ref, val_ref, out_ref, *banks):
    n = val_ref.shape[0]
    per = n // NB
    stage = banks[-NB:]
    accs = (out_ref,) + tuple(banks[:NB - 1])
    for a in accs:
        a[...] = jnp.zeros_like(a)
    def chunk(c, _):
        for k in range(NB):
            base = k * per + c * CH
            stage[k][...] = val_ref[pl.ds(pl.multiple_of(base, CH), CH), :].astype(jnp.float32)
        for j in range(CH):
            ix = [idx_ref[k * per + c * CH + j] for k in range(NB)]
            new = [accs[k][pl.ds(ix[k], 1), :] + stage[k][pl.ds(j, 1), :] for k in range(NB)]
            for k in range(NB):
                accs[k][pl.ds(ix[k], 1), :] = new[k]
        return 0
    lax.fori_loop(0, per // CH, chunk, 0)
    if NB > 1:
        tot = out_ref[...]
        for a in accs[1:]:
            tot = tot + a[...]
        out_ref[...] = tot

def rmw(idx, val, rows, NB=4, CH=16):
    return pl.pallas_call(functools.partial(rmw_kernel, NB, CH), out_shape=jax.ShapeDtypeStruct((rows,128), jnp.float32),
        in_specs=[S, V], out_specs=V, scratch_shapes=[pltpu.VMEM((rows,128), jnp.float32)]*(NB-1)+[pltpu.VMEM((CH,128), jnp.float32)]*NB,
        compiler_params=BIG, name="settle_rows")(idx, val)

def mlp_kernel(hpos, cpos, hrow, crow, bottom, labels, w1_hbm, w2_hbm, wo, hsend, csend, w1, w2, h32, c32, x, g32, sem):
    cp1 = pltpu.make_async_copy(w1_hbm, w1, sem.at[0])
    cp2 = pltpu.make_async_copy(w2_hbm, w2, sem.at[1])
    cp1.start()
    cp2.start()
    h32[...] = hrow[...].astype(jnp.float32)
    c32[...] = crow[...].astype(jnp.float32)
    UN = 16
    for f in range(8):
        def body(k, _):
            for j in range(UN):
                b = k * UN + j
                v = h32[pl.ds(hpos[2 * f, b], 1), :] + h32[pl.ds(hpos[2 * f + 1, b], 1), :] + c32[pl.ds(cpos[f, b], 1), :]
                g32[f, pl.ds(b, 1), :] = v
            return 0
        lax.fori_loop(0, 128 // UN, body, 0)
    x[:, :128] = bottom[...]
    for f in range(8):
        x[:, (f + 1) * 128:(f + 2) * 128] = g32[f].astype(jnp.bfloat16)
    h32[...] = jnp.zeros_like(h32)
    c32[...] = jnp.zeros_like(c32)
    cp1.wait()
    p1 = jnp.dot(x[...], w1[...], preferred_element_type=jnp.float32)
    a1 = jnp.maximum(p1, 0.0).astype(jnp.bfloat16)
    cp2.wait()
    p2 = jnp.dot(a1, w2[...], preferred_element_type=jnp.float32)
    a2 = jnp.maximum(p2, 0.0).astype(jnp.bfloat16)
    wof = wo[...].astype(jnp.float32)
    score = jnp.sum(a2.astype(jnp.float32) * wof, axis=1, keepdims=True)
    delta = jax.nn.sigmoid(score) - labels[...]
    g2 = jnp.where(p2 > 0, delta * wof, 0.0).astype(jnp.bfloat16)
    NT = (((1,), (1,)), ((), ()))
    b2 = lax.dot_general(g2, w2[...], NT, preferred_element_type=jnp.float32)
    g1 = jnp.where(a1 > 0, b2, 0.0).astype(jnp.bfloat16)
    for f in range(8):
        g32[f] = lax.dot_general(g1, w1[(f + 1) * 128:(f + 2) * 128, :], NT, preferred_element_type=jnp.float32)
    for f in range(8):
        def body2(k, _):
            for j in range(UN):
                b = k * UN + j
                v = g32[f, pl.ds(b, 1), :]
                h32[pl.ds(hpos[2 * f, b], 1), :] = v
                h32[pl.ds(hpos[2 * f + 1, b], 1), :] = v
                c32[pl.ds(cpos[f, b], 1), :] = v
            return 0
        lax.fori_loop(0, 128 // UN, body2, 0)
    hsend[...] = h32[...].astype(jnp.bfloat16)
    csend[...] = c32[...].astype(jnp.bfloat16)

ANY = pl.BlockSpec(memory_space=pl.ANY)
def mlp(hpos, cpos, hrow, crow, bottom, labels, w1, w2, wo):
    sh = jax.ShapeDtypeStruct((4096,128), jnp.bfloat16)
    return pl.pallas_call(mlp_kernel, out_shape=[sh, sh], in_specs=[S,S,V,V,V,V,ANY,ANY,V], out_specs=[V,V],
        scratch_shapes=[pltpu.VMEM((1152,2048), jnp.bfloat16), pltpu.VMEM((2048,2048), jnp.bfloat16),
          pltpu.VMEM((4096,128), jnp.float32), pltpu.VMEM((4096,128), jnp.float32), pltpu.VMEM((128,1152), jnp.bfloat16),
          pltpu.VMEM((8,128,128), jnp.float32), pltpu.SemaphoreType.DMA((2,))], compiler_params=BIG, name="mlp")(hpos,cpos,hrow,crow,bottom,labels,w1,w2,wo)


STEP_RATE = 0.5


def update(embedding, accum, gradient):
    new_accum = accum + jnp.mean(gradient * gradient, axis=1)
    return (embedding - STEP_RATE * gradient / jnp.sqrt(new_accum)[:, None], new_accum)


def shards(hot_table, hot_acc, cold_table, cold_acc, bottom_out, labels, hot_owner, hot_offset,
           cold_owner, cold_offset, w_first, w_second, w_out):
    def flat(x):
        return jnp.transpose(x, (1, 2, 0)).reshape(-1, 128)
    hreq, hpos, creq, cpos = place(flat(hot_owner), flat(hot_offset), flat(cold_owner), flat(cold_offset))
    def swap(x, axes):
        return lax.all_to_all(x, axes, split_axis=0, concat_axis=0, tiled=True)
    both = ("group", "member")
    hask = swap(hreq.reshape(16, 1, 256), "member").reshape(-1)
    cask = swap(creq.reshape(128, 1, 32), both).reshape(-1)
    hrow = swap(serve(hask, hot_table).reshape(16, 256, 128), "member").reshape(-1, 128)
    crow = swap(serve(cask, cold_table).reshape(128, 32, 128), both).reshape(-1, 128)
    hsend, csend = mlp(hpos, cpos, hrow, crow, bottom_out, labels.reshape(128, 1), w_first, w_second, w_out.reshape(1, -1))
    hgot = swap(hsend.reshape(16, 256, 128), "member").reshape(-1, 128)
    hot_part = settle(hask, hgot, 2048, 512, 1024)
    mine = swap(hot_part.astype(jnp.bfloat16).reshape(8, 256, 128), "group")
    total = jnp.sum(mine.astype(jnp.float32), axis=0).astype(jnp.bfloat16)
    hot_grad = swap(jnp.broadcast_to(total[None], (8, 256, 128)), "group").reshape(2048, 128).astype(jnp.float32)
    cgot = swap(csend.reshape(128, 32, 128), both).reshape(-1, 128)
    cold_grad = rmw(cask, cgot, 4096)
    new_hot, new_hot_acc = update(hot_table, hot_acc, hot_grad)
    new_cold, new_cold_acc = update(cold_table, cold_acc, cold_grad)
    return (new_hot, new_hot_acc, new_cold, new_cold_acc)


def solution(mesh):
    both = P(("group", "member"))
    in_specs = (P("member"), P("member")) + (both,) * 8 + (P(),) * 3
    out_specs = (P("member"), P("member"), both, both)
    return jax.shard_map(shards, mesh=mesh, in_specs=in_specs, out_specs=out_specs, check_vma=False)
```

time: 381 us -> 185 us (0.49)
  the two profiles are of different devices: /device:TPU:0 before, /device:TPU:1 now
where the time goes in v1:
time: 185 us; the launch traced here: 184 us
  Pallas kernels  54 us (29%)
  waiting for transfers between devices  44.8 us (24%)
  blocking collectives  35.3 us (19%)
  starting transfers between devices  33.4 us (18%)
  other arithmetic  11.1 us (6%)
  local copies, waits for them, and re-layouts  5.13 us (3%)
    all_to_all x6, waiting for transfers between devices, swap(): return lax.all_to_all(x, axes, split_axis=0, concat_axis=0, tiled=True)  44.8 us
    all_to_all x2, blocking collectives, swap(): return lax.all_to_all(x, axes, split_axis=0, concat_axis=0, tiled=True)  35.3 us
    all_to_all x6, starting transfers between devices, swap(): return lax.all_to_all(x, axes, split_axis=0, concat_axis=0, tiled=True)  33.4 us
    pallas_call x1, Pallas kernels, mlp(): pl.pallas_call(mlp_kernel, out_shape=[sh, sh], in_specs=[S, S, V, V, V, V...  19.7 us
    pallas_call x2, Pallas kernels, serve(): pl.pallas_call(functools.partial(serve_kernel, U, CH), out_shape=jax.Shap...  13.8 us
    pallas_call x1, Pallas kernels, rmw(): pl.pallas_call(functools.partial(rmw_kernel, NB, CH), out_shape=jax.Shape...  11 us
    pallas_call x1, Pallas kernels, settle(): pl.pallas_call(functools.partial(settle_kernel, BR, BK), out_shape=jax.Sh...  7.2 us
    sub x2, other arithmetic, update(): embedding - STEP_RATE * gradient / jnp.sqrt(new_accum)[:, None]  4.23 us
  transfers between devices with their start and end apart: 6, of which 5 were waited for; matrix products, arithmetic and copies ran while one was open for 6% of the time, Pallas kernels for 17%

profile of v1, /device:TPU:1, one launch (start us, length us, event | category | flops | bytes accessed | tf_op | source)
XLA Modules:
  0.0 184.5 jit_solution(588264447997870308)
XLA Ops:
  0.6 2.2 %place.1 = (s32[16,256]{1,0:T(8,128)}, s32[16,128]{1,0:T(8,128)}, s32[128,32]{1,0:T(8,128)}, s32[8,128]{1,0:T(8,128)}) custom-call(s32[16,128]{1,0:T(8,128)} %bitcast.51, s32[16,128]{1,0:T(8,128)} %bitcast.52, s32[8,128]{1,0:T(8,128)} %bitcast.53, s32[8,128]{1,0:T(8,128)} %bitcast.54), custom_call_target="tpu_custom_call" | custom-call | tf_op jit(solution)/shard_map/place/pallas_call | solution.py:45
  2.9 0.7 copy.25
  3.6 14.8 %all_to_all.40 = s32[16,1,256]{2,1,0:T(1,128)} all-to-all(s32[16,1,256]{2,1,0:T(1,128)S(1)} %copy.25), channel_id=1, replica_groups=mesh['group'=8,'member'=16] {'member'}, dimensions={0} | all-to-all | bytes 32768 | tf_op jit(solution)/shard_map/all_to_all | solution.py:182
  18.4 7.4 %all-to-all-start.2 = ((s32[128,1,32]{2,1,0:T(1,128)}), s32[128,1,32]{2,1,0:T(1,128)S(1)}, u32[]{:S(2)}, u32[]{:S(2)}) async-start(s32[128,1,32]{2,1,0:T(1,128)} %bitcast.48), calls=%async_computation.2 | async-start | bytes 131072 | tf_op jit(solution)/shard_map/all_to_all | solution.py:182
  25.8 6.7 %serve.2 = bf16[4096,128]{1,0:T(8,128)(2,1)} custom-call(s32[4096]{0:T(1024)} %bitcast.46, f32[2048,128]{1,0:T(8,128)} %tab_ref.2), custom_call_target="tpu_custom_call" | custom-call | tf_op jit(solution)/shard_map/serve/pallas_call | solution.py:59
  32.5 3.0 %all-to-all-done.2 = s32[128,1,32]{2,1,0:T(1,128)S(1)} async-done(((s32[128,1,32]{2,1,0:T(1,128)}), s32[128,1,32]{2,1,0:T(1,128)S(1)}, u32[]{:S(2)}, u32[]{:S(2)}) %all-to-all-start.2) | async-done | bytes 16416 | tf_op jit(solution)/shard_map/all_to_all | solution.py:182
  35.5 4.1 %all-to-all-start.1 = ((bf16[16,256,128]{2,1,0:T(8,128)(2,1)}), bf16[16,256,128]{2,1,0:T(8,128)(2,1)S(1)}, u32[]{:S(2)}, u32[]{:S(2)}) async-start(bf16[16,256,128]{2,1,0:T(8,128)(2,1)} %bitcast.43), calls=%async_computation.1 | async-start | bytes 2097152 | tf_op jit(solution)/shard_map/all_to_all | solution.py:182
  40.2 0.8 reduce.5
  41.0 0.7 reshape.84.idx_ref
  41.7 7.1 %serve.3 = bf16[4096,128]{1,0:T(8,128)(2,1)} custom-call(s32[4096]{0:T(1024)} %reshape.84.idx_ref, f32[4096,128]{1,0:T(8,128)} %tab_ref.3), custom_call_target="tpu_custom_call" | custom-call | tf_op jit(solution)/shard_map/serve/pallas_call | solution.py:59
  48.8 7.2 %all-to-all-done.1 = bf16[16,256,128]{2,1,0:T(8,128)(2,1)S(1)} async-done(((bf16[16,256,128]{2,1,0:T(8,128)(2,1)}), bf16[16,256,128]{2,1,0:T(8,128)(2,1)S(1)}, u32[]{:S(2)}, u32[]{:S(2)}) %all-to-all-start.1) | async-done | bytes 1048608 | tf_op jit(solution)/shard_map/all_to_all | solution.py:182
  56.0 7.3 %all-to-all-start.3 = ((bf16[128,32,128]{2,1,0:T(8,128)(2,1)}), bf16[128,32,128]{2,1,0:T(8,128)(2,1)S(1)}, u32[]{:S(2)}, u32[]{:S(2)}) async-start(bf16[128,32,128]{2,1,0:T(8,128)(2,1)} %bitcast.42), calls=%async_computation.3 | async-start | bytes 2097152 | tf_op jit(solution)/shard_map/all_to_all | solution.py:182
  63.3 0.6 reshape.88.wo
  63.9 0.7 copy.27.labels
  64.7 17.9 %all-to-all-done.3 = bf16[128,32,128]{2,1,0:T(8,128)(2,1)S(1)} async-done(((bf16[128,32,128]{2,1,0:T(8,128)(2,1)}), bf16[128,32,128]{2,1,0:T(8,128)(2,1)S(1)}, u32[]{:S(2)}, u32[]{:S(2)}) %all-to-all-start.3) | async-done | bytes 1048608 | tf_op jit(solution)/shard_map/all_to_all | solution.py:182
  82.6 1.0 copy-done.4
  83.6 19.7 %mlp.1 = (bf16[4096,128]{1,0:T(8,128)(2,1)}, bf16[4096,128]{1,0:T(8,128)(2,1)}) custom-call(s32[16,128]{1,0:T(8,128)} %get-tuple-element.11.hpos, s32[8,128]{1,0:T(8,128)} %get-tuple-element.12.cpos, bf16[4096,128]{1,0:T(8,128)(2,1)} %bitcast.39, bf16[4096,128]{1,0:T(8,128)(2,1)} %bitcast.41, bf16[128,128]{1,0:T(8,128)(2,1)} %bottom.1, ...), custom_call_target="tpu_custom_call" | custom-call | tf_op jit(solution)/shard_map/mlp/pallas_call | solution.py:162
  103.2 20.5 %all_to_all.41 = bf16[16,256,128]{2,1,0:T(8,128)(2,1)} all-to-all(bf16[16,256,128]{2,1,0:T(8,128)(2,1)} %bitcast.45), channel_id=1, replica_groups=mesh['group'=8,'member'=16] {'member'}, dimensions={0} | all-to-all | bytes 2097152 | tf_op jit(solution)/shard_map/all_to_all | solution.py:182
  123.7 5.4 %all-to-all-start.7 = ((bf16[128,32,128]{2,1,0:T(8,128)(2,1)}), bf16[128,32,128]{2,1,0:T(8,128)(2,1)S(1)}, u32[]{:S(2)}, u32[]{:S(2)}) async-start(bf16[128,32,128]{2,1,0:T(8,128)(2,1)} %bitcast.24), calls=%async_computation.7 | async-start | bytes 2097152 | tf_op jit(solution)/shard_map/all_to_all | solution.py:182
  129.1 7.2 %settle.1 = f32[2048,128]{1,0:T(8,128)} custom-call(s32[1,4096]{1,0:T(1,128)} %bitcast.47, bf16[4096,128]{1,0:T(8,128)(2,1)} %bitcast.44), custom_call_target="tpu_custom_call" | custom-call | tf_op jit(solution)/shard_map/settle/pallas_call | solution.py:78
  136.3 2.1 %convert_element_type.10 = bf16[2048,128]{1,0:T(8,128)(2,1)} convert(f32[2048,128]{1,0:T(8,128)} %settle.1) | non-fusion elementwise | flops 262144 | bytes 1572864 | tf_op jit(solution)/shard_map/convert_element_type | solution.py:191
  138.4 10.1 %all-to-all-done.7 = bf16[128,32,128]{2,1,0:T(8,128)(2,1)S(1)} async-done(((bf16[128,32,128]{2,1,0:T(8,128)(2,1)}), bf16[128,32,128]{2,1,0:T(8,128)(2,1)S(1)}, u32[]{:S(2)}, u32[]{:S(2)}) %all-to-all-start.7) | async-done | bytes 1048608 | tf_op jit(solution)/shard_map/all_to_all | solution.py:182
  148.6 4.2 %all-to-all-start.5 = ((bf16[8,256,128]{2,1,0:T(8,128)(2,1)}), bf16[8,256,128]{2,1,0:T(8,128)(2,1)S(1)}, u32[]{:S(2)}, u32[]{:S(2)}) async-start(bf16[8,256,128]{2,1,0:T(8,128)(2,1)} %bitcast.22), calls=%async_computation.5 | async-start | bytes 1048576 | tf_op jit(solution)/shard_map/all_to_all | solution.py:182
  152.8 11.0 %settle_rows.1 = f32[4096,128]{1,0:T(8,128)} custom-call(s32[4096]{0:T(1024)} %reshape.84.idx_ref, bf16[4096,128]{1,0:T(8,128)(2,1)} %bitcast.40), custom_call_target="tpu_custom_call" | custom-call | tf_op jit(solution)/shard_map/settle_rows/pallas_call | solution.py:106
  163.8 2.4 %multiply_reduce_fusion = f32[4096]{0:T(1024)S(1)} fusion(f32[4096,128]{1,0:T(8,128)} %settle_rows.1), kind=kLoop, calls=%fused_computation.1 | loop fusion | flops 1044480 | bytes 2113536 | tf_op jit(solution)/shard_map/reduce_sum | solution.py:172
  166.2 0.6 fusion.2
  166.9 0.9 broadcast_in_dim.2
  167.8 4.9 %all-to-all-start.6 = ((bf16[8,256,128]{2,1,0:T(8,128)(2,1)}), bf16[8,256,128]{2,1,0:T(8,128)(2,1)S(1)}, u32[]{:S(2)}, u32[]{:S(2)}) async-start(bf16[8,256,128]{2,1,0:T(8,128)(2,1)} %broadcast_in_dim.2), calls=%async_computation.6 | async-start | bytes 1048576 | tf_op jit(solution)/shard_map/all_to_all | solution.py:182
  172.7 2.9 %divide_subtract_fusion = f32[4096,128]{1,0:T(8,128)} fusion(f32[4096,128]{1,0:T(8,128)} %tab_ref.3, f32[4096,128]{1,0:T(8,128)S(1)} %copy-done, f32[4096]{0:T(1024)S(1)} %get-tuple-element.16), kind=kLoop, calls=%fused_computation | loop fusion | flops 1572864 | bytes 6307840 | tf_op jit(solution)/shard_map/sub | solution.py:173
  175.6 6.6 %all-to-all-done.6 = bf16[8,256,128]{2,1,0:T(8,128)(2,1)S(1)} async-done(((bf16[8,256,128]{2,1,0:T(8,128)(2,1)}), bf16[8,256,128]{2,1,0:T(8,128)(2,1)S(1)}, u32[]{:S(2)}, u32[]{:S(2)}) %all-to-all-start.6) | async-done | bytes 524320 | tf_op jit(solution)/shard_map/all_to_all | solution.py:182
  182.5 0.6 fusion.3
  183.1 1.3 fusion.1
  (23 shorter events, 1.0 us)
Async XLA Ops:
  18.4 17.1 %all-to-all-start.2 = ((s32[128,1,32]{2,1,0:T(1,128)}), s32[128,1,32]{2,1,0:T(1,128)S(1)}, u32[]{:S(2)}, u32[]{:S(2)}) async-start(s32[128,1,32]{2,1,0:T(1,128)} %bitcast.48), calls=%async_computation.2 | async-start | bytes 131072 | tf_op jit(solution)/shard_map/all_to_all | solution.py:182
  35.5 20.5 %all-to-all-start.1 = ((bf16[16,256,128]{2,1,0:T(8,128)(2,1)}), bf16[16,256,128]{2,1,0:T(8,128)(2,1)S(1)}, u32[]{:S(2)}, u32[]{:S(2)}) async-start(bf16[16,256,128]{2,1,0:T(8,128)(2,1)} %bitcast.43), calls=%async_computation.1 | async-start | bytes 2097152 | tf_op jit(solution)/shard_map/all_to_all | solution.py:182
  41.7 21.6 %copy-start.7 = (bf16[2048]{0:T(1024)(128)(2,1)S(1)}, bf16[2048]{0:T(1024)(128)(2,1)}, u32[]{:S(2)}) copy-start(bf16[2048]{0:T(1024)(128)(2,1)} %param.25) | copy-start | bytes 12292
  41.7 22.2 %copy-start.8 = (f32[128]{0:T(128)S(1)}, f32[128]{0:T(128)}, u32[]{:S(2)}) copy-start(f32[128]{0:T(128)} %param.18) | copy-start | bytes 1540
  56.0 26.6 %copy-start.2 = (bf16[16,256,128]{2,1,0:T(8,128)(2,1)}, bf16[16,256,128]{2,1,0:T(8,128)(2,1)S(1)}, u32[]{:S(2)}) copy-start(bf16[16,256,128]{2,1,0:T(8,128)(2,1)S(1)} %all-to-all-done.1) | copy-start | bytes 3145732
  56.0 26.6 %all-to-all-start.3 = ((bf16[128,32,128]{2,1,0:T(8,128)(2,1)}), bf16[128,32,128]{2,1,0:T(8,128)(2,1)S(1)}, u32[]{:S(2)}, u32[]{:S(2)}) async-start(bf16[128,32,128]{2,1,0:T(8,128)(2,1)} %bitcast.42), calls=%async_computation.3 | async-start | bytes 2097152 | tf_op jit(solution)/shard_map/all_to_all | solution.py:182
  82.6 1.0 copy-start.4
  123.7 24.8 %all-to-all-start.7 = ((bf16[128,32,128]{2,1,0:T(8,128)(2,1)}), bf16[128,32,128]{2,1,0:T(8,128)(2,1)S(1)}, u32[]{:S(2)}, u32[]{:S(2)}) async-start(bf16[128,32,128]{2,1,0:T(8,128)(2,1)} %bitcast.24), calls=%async_computation.7 | async-start | bytes 2097152 | tf_op jit(solution)/shard_map/all_to_all | solution.py:182
  148.6 4.2 %copy-start.3 = (bf16[128,32,128]{2,1,0:T(8,128)(2,1)}, bf16[128,32,128]{2,1,0:T(8,128)(2,1)S(1)}, u32[]{:S(2)}) copy-start(bf16[128,32,128]{2,1,0:T(8,128)(2,1)S(1)} %all-to-all-done.7) | copy-start | bytes 3145732
  148.6 18.3 %all-to-all-start.5 = ((bf16[8,256,128]{2,1,0:T(8,128)(2,1)}), bf16[8,256,128]{2,1,0:T(8,128)(2,1)S(1)}, u32[]{:S(2)}, u32[]{:S(2)}) async-start(bf16[8,256,128]{2,1,0:T(8,128)(2,1)} %bitcast.22), calls=%async_computation.5 | async-start | bytes 1048576 | tf_op jit(solution)/shard_map/all_to_all | solution.py:182
  152.8 13.4 %copy-start.5 = (f32[4096]{0:T(1024)S(1)}, f32[4096]{0:T(1024)}, u32[]{:S(2)}) copy-start(f32[4096]{0:T(1024)} %param.16) | copy-start | bytes 49156
  163.8 8.8 %copy-start = (f32[4096,128]{1,0:T(8,128)S(1)}, f32[4096,128]{1,0:T(8,128)}, u32[]{:S(2)}) copy-start(f32[4096,128]{1,0:T(8,128)} %settle_rows.1) | copy-start | bytes 6291460
  167.8 14.4 %all-to-all-start.6 = ((bf16[8,256,128]{2,1,0:T(8,128)(2,1)}), bf16[8,256,128]{2,1,0:T(8,128)(2,1)S(1)}, u32[]{:S(2)}, u32[]{:S(2)}) async-start(bf16[8,256,128]{2,1,0:T(8,128)(2,1)} %broadcast_in_dim.2), calls=%async_computation.6 | async-start | bytes 1048576 | tf_op jit(solution)/shard_map/all_to_all | solution.py:182
  172.7 9.9 %copy-start.6 = (f32[2048]{0:T(1024)S(1)}, f32[2048]{0:T(1024)}, u32[]{:S(2)}) copy-start(f32[2048]{0:T(1024)} %param.14) | copy-start | bytes 24580
  175.6 7.6 %copy-start.1 = (f32[2048,128]{1,0:T(8,128)S(1)}, f32[2048,128]{1,0:T(8,128)}, u32[]{:S(2)}) copy-start(f32[2048,128]{1,0:T(8,128)} %tab_ref.2) | copy-start | bytes 3145732

commit v2 on v0

v2 whole, which is shorter than its diff:
```python
import functools

import jax
import jax.numpy as jnp
from jax import lax
from jax.experimental import pallas as pl
from jax.experimental.pallas import tpu as pltpu
from jax.sharding import PartitionSpec as P

STEP_RATE = 0.5
LANES = 128
MEMBERS = 16
GROUPS = 8
DEVICES = 128
HOT_ROWS = 2048
COLD_ROWS = 4096
HCAP = 256
CCAP = 32
HIDDEN = 2048
TABLES = 8
SLICE = HOT_ROWS // GROUPS
MESH = pl.DeviceIdType.MESH
NT = (((1,), (1,)), ((), ()))

VMEM = pl.BlockSpec(memory_space=pltpu.VMEM)
SMEM = pl.BlockSpec(memory_space=pltpu.SMEM)
ANY = pl.BlockSpec(memory_space=pl.ANY)
DMA = pltpu.SemaphoreType.DMA


def f32(*shape):
    return pltpu.VMEM(shape, jnp.float32)


def b16(*shape):
    return pltpu.VMEM(shape, jnp.bfloat16)


def peer(step):
    group, member = lax.axis_index("group"), lax.axis_index("member")
    dx, dz, dc, dy = step % 4, (step // 4) % 4, (step // 16) % 2, step // 32
    to_group = (group // 2 + dy) % 4 * 2 + (group % 2 + dc) % 2
    to_member = (member // 4 + dz) % 4 * 4 + (member % 4 + dx) % 4
    return to_group, to_member


def greet_all():
    barrier = pltpu.get_barrier_semaphore()

    def signal(step, unused):
        pl.semaphore_signal(barrier, inc=1, device_id=peer(step), device_id_type=MESH)
        return unused

    lax.fori_loop(1, DEVICES, signal, 0)
    return barrier


def mixed(step):
    return step * 45 % DEVICES


def remote(src, dst, send, recv, to):
    return pltpu.make_async_remote_copy(
        src_ref=src, dst_ref=dst, send_sem=send, recv_sem=recv, device_id=to, device_id_type=MESH
    )


def place(owner_ref, offset_ref, owners, cap, request_ref, position_ref):
    rows = owner_ref.shape[0]
    owner_ids = lax.broadcasted_iota(jnp.int32, (owners, LANES), 0)
    hits = [(owner_ref[r : r + 1, :] == owner_ids).astype(jnp.float32) for r in range(rows)]
    stacked = jnp.concatenate(hits, axis=0).astype(jnp.bfloat16)
    first = lax.broadcasted_iota(jnp.int32, (LANES, LANES), 0)
    second = lax.broadcasted_iota(jnp.int32, (LANES, LANES), 1)
    earlier = (first < second).astype(jnp.float32)
    side = jnp.concatenate([earlier, jnp.ones((LANES, LANES), jnp.float32)], axis=1)
    counts = jnp.dot(stacked, side.astype(jnp.bfloat16), preferred_element_type=jnp.float32)
    base = jnp.zeros((owners, LANES), jnp.float32)
    slots = lax.broadcasted_iota(jnp.int32, (cap, LANES), 0)
    high, low, at_slot = [], [], []
    for r in range(rows):
        count = counts[r * owners : (r + 1) * owners]
        slot = jnp.sum(hits[r] * (count[:, :LANES] + base), axis=0, keepdims=True).astype(jnp.int32)
        base = base + count[:, LANES:]
        position_ref[r : r + 1, :] = owner_ref[r : r + 1, :] * cap + slot
        offset = offset_ref[r : r + 1, :]
        high.append(hits[r] * (offset // 64).astype(jnp.float32))
        low.append(hits[r] * (offset % 64).astype(jnp.float32))
        at_slot.append((slots == slot).astype(jnp.float32).astype(jnp.bfloat16))
    digits = jnp.concatenate(
        [jnp.concatenate(high, axis=1), jnp.concatenate(low, axis=1)], axis=0
    ).astype(jnp.bfloat16)
    placed = lax.dot_general(
        digits, jnp.concatenate(at_slot, axis=1), NT, preferred_element_type=jnp.float32
    )
    requests = (placed[:owners] * 64.0 + placed[owners:]).astype(jnp.int32)
    for owner in range(owners):
        request_ref[owner, :, :cap] = requests[owner : owner + 1, :]


def place_kernel(
    hot_owner, hot_offset, cold_owner, cold_offset, hot_request, hot_pos, cold_request, cold_pos
):
    cold_request[...] = jnp.zeros_like(cold_request)
    place(hot_owner, hot_offset, MEMBERS, HCAP, hot_request, hot_pos)
    place(cold_owner, cold_offset, DEVICES, CCAP, cold_request, cold_pos)


def place_all(hot_owner, hot_offset, cold_owner, cold_offset):
    shapes = [
        (MEMBERS, 1, HCAP), (2 * TABLES, LANES), (DEVICES, 1, LANES), (TABLES, LANES)
    ]
    return pl.pallas_call(
        place_kernel,
        out_shape=[jax.ShapeDtypeStruct(shape, jnp.int32) for shape in shapes],
        in_specs=[VMEM] * 4,
        out_specs=[VMEM] * 4,
        compiler_params=pltpu.CompilerParams(vmem_limit_bytes=32 << 20),
        name="place",
    )(hot_owner, hot_offset, cold_owner, cold_offset)


def fetch_kernel(
    hot_request, cold_request, hot_hbm, cold_hbm,
    hot_asked, cold_asked, hot_rows, cold_rows,
    hot_table, cold_table, hot_index, cold_index,
    hot_out, cold_out, stage, local_sem, send_sem, recv_sem,
):
    group, member = lax.axis_index("group"), lax.axis_index("member")
    me = group * MEMBERS + member
    barrier = greet_all()
    hot_load = pltpu.make_async_copy(hot_hbm, hot_table, local_sem.at[0])
    cold_load = pltpu.make_async_copy(cold_hbm, cold_table, local_sem.at[1])
    hot_load.start()
    cold_load.start()
    pl.semaphore_wait(barrier, DEVICES - 1)

    def ask_hot(step, unused):
        to = peer(step)
        remote(hot_request.at[to[1]], hot_asked.at[member], send_sem.at[0], recv_sem.at[0], to).start()
        return unused

    def ask_cold(step, unused):
        to = peer(mixed(step))
        remote(
            cold_request.at[to[0] * MEMBERS + to[1]], cold_asked.at[me],
            send_sem.at[1], recv_sem.at[1], to,
        ).start()
        return unused

    lax.fori_loop(1, MEMBERS, ask_hot, 0)
    lax.fori_loop(1, DEVICES, ask_cold, 0)
    hot_asked[member] = hot_request[member]
    cold_asked[me] = cold_request[me]

    next_peer = peer(1)

    def drain(buffer, parts, which):
        part = buffer.at[pl.ds(0, parts)]
        return remote(part, part, send_sem.at[which], recv_sem.at[which], next_peer)

    drain(hot_asked, MEMBERS - 1, 0).wait_recv()
    to_scalars = pltpu.make_async_copy(hot_asked, hot_index, local_sem.at[2])
    to_scalars.start()
    hot_load.wait()
    to_scalars.wait()

    def pick(table, index, owner, first, target):
        for j in range(CCAP):
            stage[pl.ds(j, 1), :] = table[pl.ds(index[owner, 0, first + j], 1), :]
        target[...] = stage[...].astype(jnp.bfloat16)

    def serve_hot(step, unused):
        to = peer(step)

        def chunk(c, carry):
            first = pl.multiple_of(c * CCAP, CCAP)
            pick(hot_table, hot_index, to[1], first, hot_out.at[to[1], pl.ds(first, CCAP), :])
            return carry

        lax.fori_loop(0, HCAP // CCAP, chunk, 0)
        return unused

    def serve_hot_send(step, unused):
        serve_hot(step, unused)
        to = peer(step)
        remote(hot_out.at[to[1]], hot_rows.at[member], send_sem.at[2], recv_sem.at[2], to).start()
        return unused

    lax.fori_loop(1, MEMBERS, serve_hot_send, 0)
    serve_hot(0, 0)
    hot_rows[member] = hot_out[member]

    drain(cold_asked, DEVICES - 1, 1).wait_recv()
    to_scalars = pltpu.make_async_copy(cold_asked, cold_index, local_sem.at[3])
    to_scalars.start()
    cold_load.wait()
    to_scalars.wait()

    def serve_cold_send(step, unused):
        to = peer(mixed(step))
        device = to[0] * MEMBERS + to[1]
        pick(cold_table, cold_index, device, 0, cold_out.at[device])
        remote(cold_out.at[device], cold_rows.at[me], send_sem.at[3], recv_sem.at[3], to).start()
        return unused

    lax.fori_loop(1, DEVICES, serve_cold_send, 0)
    pick(cold_table, cold_index, me, 0, cold_rows.at[me])

    drain(hot_request, MEMBERS - 1, 0).wait_send()
    drain(cold_request, DEVICES - 1, 1).wait_send()
    drain(hot_rows, MEMBERS - 1, 2).wait()
    drain(cold_rows, DEVICES - 1, 3).wait()


def fetch(hot_request, cold_request, hot_table, cold_table):
    i32 = jnp.int32
    shape = jax.ShapeDtypeStruct
    return pl.pallas_call(
        fetch_kernel,
        out_shape=[
            shape((MEMBERS, 1, HCAP), i32), shape((DEVICES, 1, LANES), i32),
            shape((MEMBERS, HCAP, LANES), jnp.bfloat16), shape((DEVICES, CCAP, LANES), jnp.bfloat16),
        ],
        in_specs=[VMEM] * 2 + [ANY] * 2,
        out_specs=[VMEM] * 4,
        scratch_shapes=[
            f32(HOT_ROWS, LANES), f32(COLD_ROWS, LANES),
            pltpu.SMEM((MEMBERS, 1, HCAP), i32), pltpu.SMEM((DEVICES, 1, LANES), i32),
            b16(MEMBERS, HCAP, LANES), b16(DEVICES, CCAP, LANES), f32(CCAP, LANES),
            DMA((4,)), DMA((4,)), DMA((4,)),
        ],
        compiler_params=pltpu.CompilerParams(
            collective_id=0, has_side_effects=True, vmem_limit_bytes=40 << 20
        ),
        name="fetch",
    )(hot_request, cold_request, hot_table, cold_table)


def network_kernel(
    hot_pos, cold_pos, hot_rows, cold_rows, bottom, labels, first_hbm, second_hbm, w_out,
    hot_send, cold_send,
    w_first, w_second, hot_wide, cold_wide, features, pooled, sem,
):
    load_first = pltpu.make_async_copy(first_hbm, w_first, sem.at[0])
    load_second = pltpu.make_async_copy(second_hbm, w_second, sem.at[1])
    load_first.start()
    load_second.start()
    hot_wide[...] = hot_rows[...].astype(jnp.float32)
    cold_wide[...] = cold_rows[...].astype(jnp.float32)
    unroll = 16
    for table in range(TABLES):

        def combine(k, unused):
            for j in range(unroll):
                b = k * unroll + j
                hot = (
                    hot_wide[pl.ds(hot_pos[2 * table, b], 1), :]
                    + hot_wide[pl.ds(hot_pos[2 * table + 1, b], 1), :]
                )
                pooled[table, pl.ds(b, 1), :] = hot + cold_wide[pl.ds(cold_pos[table, b], 1), :]
            return unused

        lax.fori_loop(0, LANES // unroll, combine, 0)
    features[:, :LANES] = bottom[...]
    for table in range(TABLES):
        features[:, (table + 1) * LANES : (table + 2) * LANES] = pooled[table].astype(jnp.bfloat16)
    hot_wide[...] = jnp.zeros_like(hot_wide)
    cold_wide[...] = jnp.zeros_like(cold_wide)
    load_first.wait()
    first_pre = jnp.dot(features[...], w_first[...], preferred_element_type=jnp.float32)
    first_act = jnp.maximum(first_pre, 0.0).astype(jnp.bfloat16)
    load_second.wait()
    second_pre = jnp.dot(first_act, w_second[...], preferred_element_type=jnp.float32)
    second_act = jnp.maximum(second_pre, 0.0).astype(jnp.bfloat16)
    out_wide = w_out[...].astype(jnp.float32)
    score = jnp.sum(second_act.astype(jnp.float32) * out_wide, axis=1, keepdims=True)
    delta = jax.nn.sigmoid(score) - labels[...]
    grad_second = jnp.where(second_pre > 0, delta * out_wide, 0.0).astype(jnp.bfloat16)
    back_second = lax.dot_general(grad_second, w_second[...], NT, preferred_element_type=jnp.float32)
    grad_first = jnp.where(first_pre > 0, back_second, 0.0).astype(jnp.bfloat16)
    for table in range(TABLES):
        pooled[table] = lax.dot_general(
            grad_first, w_first[(table + 1) * LANES : (table + 2) * LANES, :], NT,
            preferred_element_type=jnp.float32,
        )
    for table in range(TABLES):

        def spread(k, unused):
            for j in range(unroll):
                b = k * unroll + j
                term = pooled[table, pl.ds(b, 1), :]
                hot_wide[pl.ds(hot_pos[2 * table, b], 1), :] = term
                hot_wide[pl.ds(hot_pos[2 * table + 1, b], 1), :] = term
                cold_wide[pl.ds(cold_pos[table, b], 1), :] = term
            return unused

        lax.fori_loop(0, LANES // unroll, spread, 0)
    hot_send[...] = hot_wide[...].astype(jnp.bfloat16)
    cold_send[...] = cold_wide[...].astype(jnp.bfloat16)


def network(hot_pos, cold_pos, hot_rows, cold_rows, bottom, labels, w_first, w_second, w_out):
    return pl.pallas_call(
        network_kernel,
        out_shape=[
            jax.ShapeDtypeStruct(hot_rows.shape, jnp.bfloat16),
            jax.ShapeDtypeStruct(cold_rows.shape, jnp.bfloat16),
        ],
        in_specs=[SMEM, SMEM, VMEM, VMEM, VMEM, VMEM, ANY, ANY, VMEM],
        out_specs=[VMEM, VMEM],
        scratch_shapes=[
            b16(*w_first.shape), b16(*w_second.shape), f32(*hot_rows.shape), f32(*cold_rows.shape),
            b16(LANES, w_first.shape[0]), f32(TABLES, LANES, LANES), DMA((2,)),
        ],
        compiler_params=pltpu.CompilerParams(vmem_limit_bytes=48 << 20),
        name="network",
    )(hot_pos, cold_pos, hot_rows, cold_rows, bottom, labels, w_first, w_second, w_out)


def settle_kernel(
    hot_send, cold_send, hot_asked, cold_got, hot_grad,
    hot_got, partial, part_out, part_got, send_sem, recv_sem,
):
    group, member = lax.axis_index("group"), lax.axis_index("member")
    me = group * MEMBERS + member
    barrier = greet_all()
    pl.semaphore_wait(barrier, DEVICES - 1)
    half = MEMBERS // 2

    def send_hot(step, unused):
        to = peer(step)
        remote(
            hot_send.at[to[1]], hot_got.at[step], send_sem.at[0], recv_sem.at[0], to
        ).start()
        return unused

    def send_hot_late(step, unused):
        to = peer(step)
        remote(
            hot_send.at[to[1]], hot_got.at[step], send_sem.at[0], recv_sem.at[1], to
        ).start()
        return unused

    def send_cold(step, unused):
        to = peer(mixed(step))
        remote(
            cold_send.at[to[0] * MEMBERS + to[1]], cold_got.at[me], send_sem.at[1], recv_sem.at[2], to
        ).start()
        return unused

    lax.fori_loop(1, half, send_hot, 0)
    lax.fori_loop(half, MEMBERS, send_hot_late, 0)
    lax.fori_loop(1, DEVICES, send_cold, 0)
    hot_got[0] = hot_send[member]
    cold_got[me] = cold_send[me]
    next_peer = peer(1)

    def drain(buffer, first, parts, send, recv):
        part = buffer.at[pl.ds(first, parts)]
        return remote(part, part, send_sem.at[send], recv_sem.at[recv], next_peer)

    def source(step):
        return (member // 4 + 4 - step // 4) % 4 * 4 + (member % 4 + 4 - step % 4) % 4

    row_ids = lax.broadcasted_iota(jnp.int32, (SLICE, HCAP), 0)

    def add_up(first, steps, total):
        for step in steps:
            wanted = hot_asked[source(step)] - first
            chosen = jnp.where(row_ids == wanted, 1.0, 0.0).astype(jnp.bfloat16)
            total = total + jnp.dot(chosen, hot_got[step], preferred_element_type=jnp.float32)
        return total

    drain(hot_got, 1, half - 1, 0, 0).wait_recv()

    def early(block, unused):
        partial[block] = add_up(block * SLICE, range(half), jnp.zeros((SLICE, LANES), jnp.float32))
        return unused

    lax.fori_loop(0, GROUPS, early, 0)
    drain(hot_got, half, MEMBERS - half, 0, 1).wait_recv()

    def late(step, unused):
        to_group = (group // 2 + step // 2) % 4 * 2 + (group % 2 + step % 2) % 2
        total = add_up(to_group * SLICE, range(half, MEMBERS), partial[to_group])
        partial[to_group] = total
        part_out[to_group] = total.astype(jnp.bfloat16)
        return to_group

    def late_send(step, unused):
        to_group = late(step, unused)
        remote(
            part_out.at[to_group], part_got.at[step], send_sem.at[2], recv_sem.at[3],
            (to_group, member),
        ).start()
        return unused

    lax.fori_loop(1, GROUPS, late_send, 0)
    late(0, 0)
    drain(part_got, 1, GROUPS - 1, 2, 3).wait_recv()
    total = partial[group]
    for step in range(1, GROUPS):
        total = total + part_got[step].astype(jnp.float32)
    hot_grad[group] = total.astype(jnp.bfloat16)

    def share(step, unused):
        to_group = (group // 2 + step // 2) % 4 * 2 + (group % 2 + step % 2) % 2
        remote(
            hot_grad.at[group], hot_grad.at[group], send_sem.at[3], recv_sem.at[4],
            (to_group, member),
        ).start()
        return unused

    lax.fori_loop(1, GROUPS, share, 0)
    drain(hot_send, 0, MEMBERS - 1, 0, 0).wait_send()
    drain(cold_send, 0, DEVICES - 1, 1, 2).wait()
    drain(part_out, 0, GROUPS - 1, 2, 3).wait_send()
    drain(hot_grad, 0, GROUPS - 1, 3, 4).wait()


def settle(hot_send, cold_send, hot_asked):
    return pl.pallas_call(
        settle_kernel,
        out_shape=[
            jax.ShapeDtypeStruct(cold_send.shape, jnp.bfloat16),
            jax.ShapeDtypeStruct((GROUPS, SLICE, LANES), jnp.bfloat16),
        ],
        in_specs=[VMEM] * 3,
        out_specs=[VMEM] * 2,
        scratch_shapes=[
            b16(*hot_send.shape), f32(GROUPS, SLICE, LANES), b16(GROUPS, SLICE, LANES),
            b16(GROUPS, SLICE, LANES), DMA((4,)), DMA((5,)),
        ],
        compiler_params=pltpu.CompilerParams(
            collective_id=1, has_side_effects=True, vmem_limit_bytes=40 << 20
        ),
        name="settle",
    )(hot_send, cold_send, hot_asked)


BANKS = 4


def update_kernel(
    cold_index, cold_got, hot_grad, hot_acc, cold_acc, hot_hbm, cold_hbm,
    new_hot_hbm, new_hot_acc, new_cold_hbm, new_cold_acc,
    hot_table, cold_table, new_hot, new_cold, *rest,
):
    banks, stages, sem = rest[:BANKS], rest[BANKS : 2 * BANKS], rest[2 * BANKS]
    load_hot = pltpu.make_async_copy(hot_hbm, hot_table, sem.at[0])
    load_cold = pltpu.make_async_copy(cold_hbm, cold_table, sem.at[1])
    load_hot.start()
    load_cold.start()
    first = lax.broadcasted_iota(jnp.int32, (LANES, LANES), 0)
    second = lax.broadcasted_iota(jnp.int32, (LANES, LANES), 1)
    diagonal = first == second

    def step(block, table, acc, new_table, new_acc, gradient):
        rows = pl.ds(pl.multiple_of(block * LANES, LANES), LANES)
        spread_acc = jnp.where(diagonal, acc[pl.ds(block, 1), :], 0.0)
        new = jnp.sum(gradient * gradient * (1.0 / LANES) + spread_acc, axis=1, keepdims=True)
        new_table[rows, :] = table[rows, :] - STEP_RATE * gradient * lax.rsqrt(new)
        new_acc[pl.ds(block, 1), :] = jnp.sum(jnp.where(diagonal, new, 0.0), axis=0, keepdims=True)

    load_hot.wait()

    def hot_block(block, unused):
        slice_rows = pl.ds(pl.multiple_of(block % 2 * LANES, LANES), LANES)
        gradient = hot_grad[block // 2, slice_rows, :].astype(jnp.float32)
        step(block, hot_table, hot_acc, new_hot, new_hot_acc, gradient)
        return unused

    lax.fori_loop(0, HOT_ROWS // LANES, hot_block, 0)
    store_hot = pltpu.make_async_copy(new_hot, new_hot_hbm, sem.at[2])
    store_hot.start()

    for bank in banks:
        bank[...] = jnp.zeros_like(bank)
    per_bank = DEVICES // BANKS

    def add_rows(c, unused):
        for k in range(BANKS):
            stages[k][...] = cold_got[k * per_bank + c].astype(jnp.float32)
        for j in range(CCAP):
            at = [cold_index[k * per_bank + c, 0, j] for k in range(BANKS)]
            new = [banks[k][pl.ds(at[k], 1), :] + stages[k][pl.ds(j, 1), :] for k in range(BANKS)]
            for k in range(BANKS):
                banks[k][pl.ds(at[k], 1), :] = new[k]
        return unused

    lax.fori_loop(0, per_bank, add_rows, 0)
    load_cold.wait()

    def cold_block(block, unused):
        rows = pl.ds(pl.multiple_of(block * LANES, LANES), LANES)
        gradient = banks[0][rows, :]
        for bank in banks[1:]:
            gradient = gradient + bank[rows, :]
        step(block, cold_table, cold_acc, new_cold, new_cold_acc, gradient)
        return unused

    lax.fori_loop(0, COLD_ROWS // LANES, cold_block, 0)
    store_cold = pltpu.make_async_copy(new_cold, new_cold_hbm, sem.at[3])
    store_cold.start()
    store_hot.wait()
    store_cold.wait()


def update(cold_index, cold_got, hot_grad, hot_acc, cold_acc, hot_table, cold_table):
    shape = jax.ShapeDtypeStruct
    return pl.pallas_call(
        update_kernel,
        out_shape=[
            shape(hot_table.shape, jnp.float32), shape(hot_acc.shape, jnp.float32),
            shape(cold_table.shape, jnp.float32), shape(cold_acc.shape, jnp.float32),
        ],
        in_specs=[SMEM] + [VMEM] * 4 + [ANY] * 2,
        out_specs=[ANY, VMEM, ANY, VMEM],
        scratch_shapes=[
            f32(HOT_ROWS, LANES), f32(COLD_ROWS, LANES), f32(HOT_ROWS, LANES), f32(COLD_ROWS, LANES),
        ] + [f32(COLD_ROWS, LANES)] * BANKS + [f32(CCAP, LANES)] * BANKS + [DMA((4,))],
        compiler_params=pltpu.CompilerParams(vmem_limit_bytes=48 << 20),
        name="update",
    )(cold_index, cold_got, hot_grad, hot_acc, cold_acc, hot_table, cold_table)


def shards(
    hot_table, hot_acc, cold_table, cold_acc, bottom_out, labels,
    hot_owner, hot_offset, cold_owner, cold_offset, w_first, w_second, w_out,
):
    def by_lane(lookups):
        return jnp.transpose(lookups, (1, 2, 0)).reshape(-1, LANES)

    hot_request, hot_pos, cold_request, cold_pos = place_all(
        by_lane(hot_owner), by_lane(hot_offset), by_lane(cold_owner), by_lane(cold_offset)
    )
    hot_asked, cold_asked, hot_rows, cold_rows = fetch(
        hot_request, cold_request, hot_table, cold_table
    )
    hot_send, cold_send = network(
        hot_pos, cold_pos, hot_rows.reshape(-1, LANES), cold_rows.reshape(-1, LANES), bottom_out,
        labels.reshape(-1, 1), w_first, w_second, w_out.reshape(1, -1),
    )
    cold_got, hot_grad = settle(
        hot_send.reshape(MEMBERS, HCAP, LANES), cold_send.reshape(DEVICES, CCAP, LANES), hot_asked
    )
    new_hot, new_hot_acc, new_cold, new_cold_acc = update(
        cold_asked, cold_got, hot_grad, hot_acc.reshape(-1, LANES), cold_acc.reshape(-1, LANES),
        hot_table, cold_table,
    )
    return (new_hot, new_hot_acc.reshape(-1), new_cold, new_cold_acc.reshape(-1))


def solution(mesh):
    both = P(("group", "member"))
    in_specs = (P("member"), P("member")) + (both,) * 8 + (P(),) * 3
    out_specs = (P("member"), P("member"), both, both)
    return jax.shard_map(shards, mesh=mesh, in_specs=in_specs, out_specs=out_specs, check_vma=False)
```

time: 381 us -> 145 us (0.38)
  the two profiles are of different devices: /device:TPU:0 before, /device:TPU:1 now
where the time goes in v2:
time: 145 us
  Pallas kernels  136 us (94%)
  local copies, waits for them, and re-layouts  7.79 us (5%)
    pallas_call x1, Pallas kernels, fetch(): pl.pallas_call(fetch_kernel, out_shape=[shape((MEMBERS, 1, HCAP), i32), s...  51 us
    pallas_call x1, Pallas kernels, settle(): pl.pallas_call(settle_kernel, out_shape=[jax.ShapeDtypeStruct(cold_send.s...  50.1 us
    pallas_call x1, Pallas kernels, network(): pl.pallas_call(network_kernel, out_shape=[jax.ShapeDtypeStruct(hot_rows.s...  17.6 us
    pallas_call x1, Pallas kernels, update(): pl.pallas_call(update_kernel, out_shape=[shape(hot_table.shape, jnp.float...  16.6 us
    unnamed x22, local copies, waits for them, and re-layouts  6.34 us

profile of v2, /device:TPU:1, one launch (start us, length us, event | category | flops | bytes accessed | tf_op | source)
XLA Modules:
  0.0 144.6 jit_solution(11839399503005298486)
XLA Ops:
  0.6 0.7 reshape.57.w_out
  1.3 0.8 copy.19.labels
  2.1 0.0 copy-start.7
  2.1 0.7 copy-done.7
  2.8 0.0 copy-start.8
  2.8 0.7 copy-done.8
  3.5 0.0 copy-start.9
  3.5 0.7 copy-done.9
  4.2 0.0 copy-start.10
  4.2 0.7 copy-done.10
  4.9 0.9 place.1
  5.7 0.0 copy-start
  5.8 1.6 %copy-done = f32[4096,128]{1,0:T(8,128)S(1)} copy-done((f32[4096,128]{1,0:T(8,128)S(1)}, f32[4096,128]{1,0:T(8,128)}, u32[]{:S(2)}) %copy-start) | copy-done | bytes 2097176
  7.3 0.0 copy-start.2
  7.3 1.2 copy-done.2
  8.6 51.0 %fetch.1 = (s32[16,1,256]{2,1,0:T(1,128)S(1)}, s32[128,1,128]{2,1,0:T(1,128)S(1)}, bf16[16,256,128]{2,1,0:T(8,128)(2,1)S(1)}, bf16[128,32,128]{2,1,0:T(8,128)(2,1)S(1)}) custom-call(s32[16,1,256]{2,1,0:T(1,128)S(1)} %get-tuple-element.20.hot_request, s32[128,1,128]{2,1,0:T(1,128)S(1)} %get-tuple-element.21.cold_request, f32[2048,128]{1,0:T(8,128)S(1)} %copy-done.2, ...), custom_call_target="tpu_custom_call" | custom-call | tf_op jit(solution)/shard_map/fetch/pallas_call | solution.py:219
  59.5 0.0 copy-start.4
  59.5 0.7 copy-done.4
  60.3 0.0 copy-start.1
  60.3 0.0 copy-start.3
  60.3 0.0 copy-start.5
  60.3 0.0 copy-start.6
  60.3 17.6 %network.1 = (bf16[4096,128]{1,0:T(8,128)(2,1)S(1)}, bf16[4096,128]{1,0:T(8,128)(2,1)S(1)}) custom-call(s32[16,128]{1,0:T(8,128)S(1)} %get-tuple-element.23.hot_pos, s32[8,128]{1,0:T(8,128)S(1)} %get-tuple-element.24.cold_pos, bf16[4096,128]{1,0:T(8,128)(2,1)S(1)} %bitcast.25, bf16[4096,128]{1,0:T(8,128)(2,1)S(1)} %bitcast.26, ...), custom_call_target="tpu_custom_call" | custom-call | tf_op jit(solution)/shard_map/network/pallas_call | solution.py:304
  77.9 50.1 %settle.1 = (bf16[128,32,128]{2,1,0:T(8,128)(2,1)S(1)}, bf16[8,256,128]{2,1,0:T(8,128)(2,1)S(1)}) custom-call(bf16[16,256,128]{2,1,0:T(8,128)(2,1)S(1)} %bitcast.27, bf16[128,32,128]{2,1,0:T(8,128)(2,1)S(1)} %bitcast.28, s32[16,1,256]{2,1,0:T(1,128)S(1)} %get-tuple-element.29.hot_asked), custom_call_target="tpu_custom_call" | custom-call | tf_op jit(solution)/shard_map/settle/pallas_call | solution.py:423
  128.0 0.0 copy-done.1
  128.1 0.0 copy-done.3
  128.1 0.0 copy-done.5
  128.1 0.0 copy-done.6
  128.1 16.6 %update.1 = (f32[2048,128]{1,0:T(8,128)}, f32[16,128]{1,0:T(8,128)}, f32[4096,128]{1,0:T(8,128)}, f32[32,128]{1,0:T(8,128)}) custom-call(s32[128,1,128]{2,1,0:T(1,128)S(1)} %get-tuple-element.22.cold_index, bf16[128,32,128]{2,1,0:T(8,128)(2,1)S(1)} %get-tuple-element.30.cold_got, bf16[8,256,128]{2,1,0:T(8,128)(2,1)S(1)} %get-tuple-element.31.hot_grad, ...), custom_call_target="tpu_custom_call" | custom-call | tf_op jit(solution)/shard_map/update/pallas_call | solution.py:512
Async XLA Ops:
  2.1 0.7 copy-start.7
  2.8 0.7 copy-start.8
  3.5 0.7 copy-start.9
  4.2 0.7 copy-start.10
  5.7 1.6 %copy-start = (f32[4096,128]{1,0:T(8,128)S(1)}, f32[4096,128]{1,0:T(8,128)}, u32[]{:S(2)}) copy-start(f32[4096,128]{1,0:T(8,128)} %cold_hbm.3) | copy-start | bytes 6291460
  7.3 1.2 copy-start.2
  59.5 0.8 copy-start.4
  60.3 67.8 %copy-start.1 = (f32[4096,128]{1,0:T(8,128)S(1)}, f32[4096,128]{1,0:T(8,128)}, u32[]{:S(2)}) copy-start(f32[4096,128]{1,0:T(8,128)} %cold_hbm.3) | copy-start | bytes 6291460
  60.3 67.8 %copy-start.3 = (f32[2048,128]{1,0:T(8,128)S(1)}, f32[2048,128]{1,0:T(8,128)}, u32[]{:S(2)}) copy-start(f32[2048,128]{1,0:T(8,128)} %hot_hbm.3) | copy-start | bytes 3145732
  60.3 67.8 %copy-start.5 = (f32[4096]{0:T(1024)S(1)}, f32[4096]{0:T(1024)}, u32[]{:S(2)}) copy-start(f32[4096]{0:T(1024)} %param.16) | copy-start | bytes 49156
  60.3 67.8 %copy-start.6 = (f32[2048]{0:T(1024)S(1)}, f32[2048]{0:T(1024)}, u32[]{:S(2)}) copy-start(f32[2048]{0:T(1024)} %param.14) | copy-start | bytes 24580

commit v3 on v0

v3 whole, which is shorter than its diff:
```python
import functools

import jax
import jax.numpy as jnp
from jax import lax
from jax.experimental import pallas as pl
from jax.experimental.pallas import tpu as pltpu
from jax.sharding import PartitionSpec as P

STEP_RATE = 0.5
LANES = 128
MEMBERS = 16
GROUPS = 8
DEVICES = 128
HOT_ROWS = 2048
COLD_ROWS = 4096
HCAP = 256
CCAP = 32
HIDDEN = 2048
TABLES = 8
SLICE = HOT_ROWS // GROUPS
MESH = pl.DeviceIdType.MESH
NT = (((1,), (1,)), ((), ()))

VMEM = pl.BlockSpec(memory_space=pltpu.VMEM)
ANY = pl.BlockSpec(memory_space=pl.ANY)
DMA = pltpu.SemaphoreType.DMA


def f32(*shape):
    return pltpu.VMEM(shape, jnp.float32)


def b16(*shape):
    return pltpu.VMEM(shape, jnp.bfloat16)


def remote(src, dst, send, recv, to):
    return pltpu.make_async_remote_copy(
        src_ref=src, dst_ref=dst, send_sem=send, recv_sem=recv, device_id=to, device_id_type=MESH
    )


def place(owner_ref, offset_ref, owners, cap, request_ref, position_ref):
    rows = owner_ref.shape[0]
    owner_ids = lax.broadcasted_iota(jnp.int32, (owners, LANES), 0)
    hits = [(owner_ref[r : r + 1, :] == owner_ids).astype(jnp.float32) for r in range(rows)]
    stacked = jnp.concatenate(hits, axis=0).astype(jnp.bfloat16)
    first = lax.broadcasted_iota(jnp.int32, (LANES, LANES), 0)
    second = lax.broadcasted_iota(jnp.int32, (LANES, LANES), 1)
    earlier = (first < second).astype(jnp.float32)
    side = jnp.concatenate([earlier, jnp.ones((LANES, LANES), jnp.float32)], axis=1)
    counts = jnp.dot(stacked, side.astype(jnp.bfloat16), preferred_element_type=jnp.float32)
    base = jnp.zeros((owners, LANES), jnp.float32)
    width = request_ref.shape[2]
    slots = lax.broadcasted_iota(jnp.int32, (width, LANES), 0) % cap
    high, low, at_slot = [], [], []
    for r in range(rows):
        count = counts[r * owners : (r + 1) * owners]
        slot = jnp.sum(hits[r] * (count[:, :LANES] + base), axis=0, keepdims=True).astype(jnp.int32)
        base = base + count[:, LANES:]
        position_ref[r : r + 1, :] = owner_ref[r : r + 1, :] * cap + slot
        offset = offset_ref[r : r + 1, :]
        high.append(hits[r] * (offset // 64).astype(jnp.float32))
        low.append(hits[r] * (offset % 64).astype(jnp.float32))
        at_slot.append((slots == slot).astype(jnp.float32).astype(jnp.bfloat16))
    digits = jnp.concatenate(
        [jnp.concatenate(high, axis=1), jnp.concatenate(low, axis=1)], axis=0
    ).astype(jnp.bfloat16)
    placed = lax.dot_general(
        digits, jnp.concatenate(at_slot, axis=1), NT, preferred_element_type=jnp.float32
    )
    requests = (placed[:owners] * 64.0 + placed[owners:]).astype(jnp.int32)
    for owner in range(owners):
        request_ref[owner] = requests[owner : owner + 1, :]


def place_kernel(
    hot_owner, hot_offset, cold_owner, cold_offset, hot_request, hot_pos, cold_request, cold_pos
):
    place(hot_owner, hot_offset, MEMBERS, HCAP, hot_request, hot_pos)
    place(cold_owner, cold_offset, DEVICES, CCAP, cold_request, cold_pos)


def place_all(hot_owner, hot_offset, cold_owner, cold_offset):
    shapes = [
        (MEMBERS, 1, HCAP), (2 * TABLES, LANES), (DEVICES, 1, LANES), (TABLES, LANES)
    ]
    return pl.pallas_call(
        place_kernel,
        out_shape=[jax.ShapeDtypeStruct(shape, jnp.int32) for shape in shapes],
        in_specs=[VMEM] * 4,
        out_specs=[VMEM] * 4,
        compiler_params=pltpu.CompilerParams(vmem_limit_bytes=32 << 20),
        name="place",
    )(hot_owner, hot_offset, cold_owner, cold_offset)


WAVES = 8
PAIRS = TABLES * LANES


def step_kernel(
    hot_request, cold_request, hot_pos, cold_pos, bottom, labels, w_out,
    hot_hbm, cold_hbm, first_hbm, second_hbm,
    hot_grad, cold_grad,
    hot_table, cold_table, w_first, w_second,
    hot_asked, cold_asked, hot_index, cold_index, hot_at, cold_at,
    hot_out, cold_out, hot_rows, cold_rows, stage, hot_wide, cold_wide, features, pooled, terms,
    hot_send, cold_send, hot_got, cold_got, partial, part_out, part_got,
    local_sem, send_sem, recv_sem, cold_sem,
):
    group, member = lax.axis_index("group"), lax.axis_index("member")
    me = group * MEMBERS + member
    z, x, y, core = lax.div(member, 4), lax.rem(member, 4), lax.div(group, 2), lax.rem(group, 2)
    xs = [lax.rem(x + d, 4) for d in range(4)]
    zs = [lax.rem(z + d, 4) * 4 for d in range(4)]
    members = [zs[d // 4] + xs[d % 4] for d in range(MEMBERS)]
    ys = [lax.rem(y + d, 4) * 2 for d in range(4)]
    cores = [core, 1 - core]
    to_group = [ys[k // 2] + cores[k % 2] for k in range(GROUPS)]
    from_group = [ys[(4 - k // 2) % 4] + cores[k % 2] for k in range(GROUPS)]

    def member_step(i):
        step = lax.rem(i * 7, MEMBERS)
        return lax.div(step, 4), lax.rem(step, 4)

    def to_member(i):
        dz, dx = member_step(i)
        return lax.rem(z + dz, 4) * 4 + lax.rem(x + dx, 4)

    def from_member(i):
        dz, dx = member_step(i)
        return lax.rem(z + 4 - dz, 4) * 4 + lax.rem(x + 4 - dx, 4)

    barrier = pltpu.get_barrier_semaphore()
    for k in range(GROUPS):
        for d in range(MEMBERS):
            if k or d:
                pl.semaphore_signal(
                    barrier, inc=1, device_id=(to_group[k], members[d]), device_id_type=MESH
                )
    loads = [
        pltpu.make_async_copy(src, dst, local_sem.at[n])
        for n, (src, dst) in enumerate(
            [
                (hot_hbm, hot_table), (cold_hbm, cold_table), (first_hbm, w_first),
                (second_hbm, w_second), (hot_pos, hot_at), (cold_pos, cold_at),
            ]
        )
    ]
    for load in loads:
        load.start()
    pl.semaphore_wait(barrier, DEVICES - 1)

    beside = (group, members[1])

    def drain(buffer, first, parts, send, recv):
        part = buffer.at[pl.ds(first, parts)]
        return remote(part, part, send, recv, beside)

    def ask_hot(i, unused):
        to = to_member(i)
        remote(
            hot_request.at[to], hot_asked.at[i], send_sem.at[0], recv_sem.at[0], (group, to)
        ).start()
        return unused

    lax.fori_loop(1, MEMBERS, ask_hot, 0)

    def ask_cold_at(i, groups):
        to = to_member(i)
        for k in groups:
            remote(
                cold_request.at[to_group[k] * MEMBERS + to], cold_asked.at[i * GROUPS + k],
                send_sem.at[1], recv_sem.at[1], (to_group[k], to),
            ).start()

    def ask_cold(i, unused):
        ask_cold_at(i, range(GROUPS))
        return unused

    ask_cold_at(0, range(1, GROUPS))
    lax.fori_loop(1, MEMBERS, ask_cold, 0)
    hot_asked[0] = hot_request[member]
    cold_asked[0] = cold_request[me]

    drain(hot_asked, 1, MEMBERS - 1, send_sem.at[0], recv_sem.at[0]).wait_recv()
    to_scalars = pltpu.make_async_copy(hot_asked, hot_index, local_sem.at[6])
    to_scalars.start()
    loads[0].wait()
    to_scalars.wait()

    def pick(table, index, row, first, target):
        for j in range(CCAP):
            stage[pl.ds(j, 1), :] = table[pl.ds(index[row, 0, first + j], 1), :]
        target[...] = stage[...].astype(jnp.bfloat16)

    def serve_hot(i, target):
        def chunk(c, unused):
            first = pl.multiple_of(c * CCAP, CCAP)
            pick(hot_table, hot_index, i, first, target.at[pl.ds(first, CCAP), :])
            return unused

        lax.fori_loop(0, HCAP // CCAP, chunk, 0)

    def serve_hot_send(i, unused):
        to = from_member(i)
        serve_hot(i, hot_out.at[i])
        remote(
            hot_out.at[i], hot_rows.at[member], send_sem.at[2], recv_sem.at[2], (group, to)
        ).start()
        return unused

    lax.fori_loop(1, MEMBERS, serve_hot_send, 0)
    serve_hot(0, hot_rows.at[member])

    drain(cold_asked, 1, DEVICES - 1, send_sem.at[1], recv_sem.at[1]).wait_recv()
    to_scalars = pltpu.make_async_copy(cold_asked, cold_index, local_sem.at[7])
    to_scalars.start()
    loads[1].wait()
    to_scalars.wait()

    def serve_cold_at(i, groups):
        to = from_member(i)
        for k in groups:
            n = i * GROUPS + k
            pick(cold_table, cold_index, n, 0, cold_out.at[n])
            remote(
                cold_out.at[n], cold_rows.at[me], send_sem.at[3], recv_sem.at[3],
                (from_group[k], to),
            ).start()

    def serve_cold(i, unused):
        serve_cold_at(i, range(GROUPS))
        return unused

    serve_cold_at(0, range(1, GROUPS))
    lax.fori_loop(1, MEMBERS, serve_cold, 0)
    pick(cold_table, cold_index, 0, 0, cold_rows.at[me])

    loads[4].wait()
    loads[5].wait()
    drain(hot_rows, 0, MEMBERS - 1, send_sem.at[2], recv_sem.at[2]).wait_recv()
    hot_wide[...] = hot_rows[...].astype(jnp.float32).reshape(hot_wide.shape)
    features[:, :LANES] = bottom[...]
    drain(cold_rows, 0, DEVICES - 1, send_sem.at[3], recv_sem.at[3]).wait_recv()
    cold_wide[...] = cold_rows[...].astype(jnp.float32).reshape(cold_wide.shape)
    unroll = 16
    for table in range(TABLES):

        def combine(k, unused):
            for j in range(unroll):
                b = k * unroll + j
                hot = (
                    hot_wide[pl.ds(hot_at[2 * table, b], 1), :]
                    + hot_wide[pl.ds(hot_at[2 * table + 1, b], 1), :]
                )
                pooled[table, pl.ds(b, 1), :] = hot + cold_wide[pl.ds(cold_at[table, b], 1), :]
            return unused

        lax.fori_loop(0, LANES // unroll, combine, 0)
        features[:, (table + 1) * LANES : (table + 2) * LANES] = pooled[table].astype(jnp.bfloat16)

    loads[2].wait()
    first_pre = jnp.dot(features[...], w_first[...], preferred_element_type=jnp.float32)
    first_act = jnp.maximum(first_pre, 0.0).astype(jnp.bfloat16)
    loads[3].wait()
    second_pre = jnp.dot(first_act, w_second[...], preferred_element_type=jnp.float32)
    second_act = jnp.maximum(second_pre, 0.0).astype(jnp.bfloat16)
    out_wide = w_out[...].astype(jnp.float32)
    score = jnp.sum(second_act.astype(jnp.float32) * out_wide, axis=1, keepdims=True)
    row_id = lax.broadcasted_iota(jnp.int32, (LANES, LANES), 0)
    lane_id = lax.broadcasted_iota(jnp.int32, (LANES, LANES), 1)
    label = jnp.sum(jnp.where(row_id == lane_id, labels[...], 0.0), axis=1, keepdims=True)
    delta = jax.nn.sigmoid(score) - label
    grad_second = jnp.where(second_pre > 0, delta * out_wide, 0.0).astype(jnp.bfloat16)
    back_second = lax.dot_general(grad_second, w_second[...], NT, preferred_element_type=jnp.float32)
    grad_first = jnp.where(first_pre > 0, back_second, 0.0).astype(jnp.bfloat16)
    for table in range(TABLES):
        terms[table * LANES : (table + 1) * LANES, :] = lax.dot_general(
            grad_first, w_first[(table + 1) * LANES : (table + 2) * LANES, :], NT,
            preferred_element_type=jnp.float32,
        ).astype(jnp.bfloat16)

    slot_id = lax.broadcasted_iota(jnp.int32, (HCAP, LANES), 0)

    def one_hot(rows, wanted):
        return jnp.concatenate([jnp.where(rows == w, 1.0, 0.0).astype(jnp.bfloat16) for w in wanted], axis=1)

    def spread_hot(to):
        base = to * HCAP
        wanted = []
        for table in range(TABLES):
            one = hot_pos[2 * table : 2 * table + 1, :] - base
            two = hot_pos[2 * table + 1 : 2 * table + 2, :] - base
            wanted.append(jnp.where((one >= 0) & (one < HCAP), one, two))
        return jnp.dot(
            one_hot(slot_id, wanted), terms[...], preferred_element_type=jnp.float32
        ).astype(jnp.bfloat16)

    def spread_hot_send(wave):
        def send(i, unused):
            to = to_member(i)
            hot_send[i] = spread_hot(to)
            remote(
                hot_send.at[i], hot_got.at[i], send_sem.at[4], recv_sem.at[4 + wave], (group, to)
            ).start()
            return unused

        return send

    half = MEMBERS // 2
    lax.fori_loop(1, half, spread_hot_send(0), 0)
    lax.fori_loop(half, MEMBERS, spread_hot_send(1), 0)
    hot_got[0] = spread_hot(member)

    def spread_cold(i):
        to = to_member(i)
        rows = jnp.concatenate(
            [slot_id[:CCAP] + (to_group[k] * MEMBERS + to) * CCAP for k in range(GROUPS)], axis=0
        )
        wanted = [cold_pos[table : table + 1, :] for table in range(TABLES)]
        sent = jnp.dot(one_hot(rows, wanted), terms[...], preferred_element_type=jnp.float32)
        cold_send[i] = sent.astype(jnp.bfloat16).reshape(GROUPS, CCAP, LANES)
        return to

    def send_cold(i, to, groups):
        wave = lax.div(i, MEMBERS // WAVES)
        for k in groups:
            remote(
                cold_send.at[i, k], cold_got.at[i * GROUPS + k], send_sem.at[5], cold_sem.at[wave],
                (to_group[k], to),
            ).start()

    def spread_cold_send(i, unused):
        send_cold(i, spread_cold(i), range(GROUPS))
        return unused

    send_cold(0, spread_cold(0), range(1, GROUPS))
    cold_got[0] = cold_send[0, 0]
    lax.fori_loop(1, half, spread_cold_send, 0)

    def add_hot(first, steps, total):
        for i in steps:
            asked = hot_asked[i] - first
            wanted = [asked[:, c * LANES : (c + 1) * LANES] for c in range(HCAP // LANES)]
            total = total + jnp.dot(
                one_hot(slot_id, wanted), hot_got[i], preferred_element_type=jnp.float32
            )
        return total

    drain(hot_got, 1, half - 1, send_sem.at[4], recv_sem.at[4]).wait_recv()

    def early(block, unused):
        partial[block] = add_hot(block * SLICE, range(half), jnp.zeros((SLICE, LANES), jnp.float32))
        return unused

    lax.fori_loop(0, GROUPS, early, 0)
    lax.fori_loop(half, MEMBERS, spread_cold_send, 0)
    drain(hot_got, half, MEMBERS - half, send_sem.at[4], recv_sem.at[5]).wait_recv()
    for k in list(range(1, GROUPS)) + [0]:
        to = to_group[k]
        total = add_hot(to * SLICE, range(half, MEMBERS), partial[to])
        if k == 0:
            own = total
        else:
            part_out[k] = total.astype(jnp.bfloat16)
            remote(
                part_out.at[k], part_got.at[k], send_sem.at[6], recv_sem.at[6], (to, member)
            ).start()
    partial[0] = own

    block_rows = 512
    per_wave = DEVICES // WAVES
    big_id = lax.broadcasted_iota(jnp.int32, (block_rows, LANES), 0)
    quarter = lax.div(lax.broadcasted_iota(jnp.int32, (1, LANES), 1), CCAP)

    def settle_cold(wave, first_wave):
        asked = []
        for c in range(per_wave // 4):
            row = cold_asked[wave * per_wave + 4 * c]
            for q in range(1, 4):
                row = jnp.where(quarter == q, cold_asked[wave * per_wave + 4 * c + q], row)
            asked.append(row)
        values = cold_got[pl.ds(wave * per_wave, per_wave)].reshape(per_wave * CCAP, LANES)

        def block(n, unused):
            first = pl.multiple_of(n * block_rows, block_rows)
            rows = pl.ds(first, block_rows)
            sums = jnp.dot(
                one_hot(big_id + first, asked), values, preferred_element_type=jnp.float32
            )
            cold_grad[rows, :] = sums if first_wave else cold_grad[rows, :] + sums
            return unused

        lax.fori_loop(0, COLD_ROWS // block_rows, block, 0)

    def cold_wave(wave, unused):
        drain(cold_got, wave * per_wave, per_wave, send_sem.at[5], cold_sem.at[wave]).wait_recv()
        settle_cold(wave, False)
        return unused

    drain(cold_got, 1, per_wave - 1, send_sem.at[5], cold_sem.at[0]).wait_recv()
    settle_cold(0, True)
    lax.fori_loop(1, 4, cold_wave, 0)

    drain(part_got, 1, GROUPS - 1, send_sem.at[6], recv_sem.at[6]).wait_recv()
    total = partial[0]
    for k in range(1, GROUPS):
        total = total + part_got[k].astype(jnp.float32)
    hot_grad[group] = total.astype(jnp.bfloat16)
    for k in range(1, GROUPS):
        remote(
            hot_grad.at[group], hot_grad.at[group], send_sem.at[7], recv_sem.at[7],
            (to_group[k], member),
        ).start()
    lax.fori_loop(4, WAVES, cold_wave, 0)

    drain(hot_asked, 1, MEMBERS - 1, send_sem.at[0], recv_sem.at[0]).wait_send()
    drain(cold_asked, 1, DEVICES - 1, send_sem.at[1], recv_sem.at[1]).wait_send()
    drain(hot_out, 1, MEMBERS - 1, send_sem.at[2], recv_sem.at[2]).wait_send()
    drain(cold_out, 1, DEVICES - 1, send_sem.at[3], recv_sem.at[3]).wait_send()
    drain(hot_send, 1, MEMBERS - 1, send_sem.at[4], recv_sem.at[4]).wait_send()
    drain(cold_got, 1, DEVICES - 1, send_sem.at[5], recv_sem.at[4]).wait_send()
    drain(part_out, 1, GROUPS - 1, send_sem.at[6], recv_sem.at[6]).wait_send()
    drain(hot_grad, 1, GROUPS - 1, send_sem.at[7], recv_sem.at[7]).wait()


def train(
    hot_request, cold_request, hot_pos, cold_pos, bottom, labels, w_out,
    hot_table, cold_table, w_first, w_second,
):
    i32 = jnp.int32
    hot_block, cold_block = (MEMBERS, HCAP, LANES), (DEVICES, CCAP, LANES)
    return pl.pallas_call(
        step_kernel,
        out_shape=[
            jax.ShapeDtypeStruct((GROUPS, SLICE, LANES), jnp.bfloat16),
            jax.ShapeDtypeStruct((COLD_ROWS, LANES), jnp.float32),
        ],
        in_specs=[VMEM] * 7 + [ANY] * 4,
        out_specs=[VMEM] * 2,
        scratch_shapes=[
            f32(HOT_ROWS, LANES), f32(COLD_ROWS, LANES), b16(*w_first.shape), b16(*w_second.shape),
            pltpu.VMEM((MEMBERS, 1, HCAP), i32), pltpu.VMEM((DEVICES, 1, LANES), i32),
            pltpu.SMEM((MEMBERS, 1, HCAP), i32), pltpu.SMEM((DEVICES, 1, LANES), i32),
            pltpu.SMEM((2 * TABLES, LANES), i32), pltpu.SMEM((TABLES, LANES), i32),
            b16(*hot_block), b16(*cold_block), b16(*hot_block), b16(*cold_block), f32(CCAP, LANES),
            f32(MEMBERS * HCAP, LANES), f32(DEVICES * CCAP, LANES),
            b16(LANES, w_first.shape[0]), f32(TABLES, LANES, LANES), b16(PAIRS, LANES),
            b16(*hot_block), b16(MEMBERS, GROUPS, CCAP, LANES), b16(*hot_block), b16(*cold_block),
            f32(GROUPS, SLICE, LANES), b16(GROUPS, SLICE, LANES), b16(GROUPS, SLICE, LANES),
            DMA((8,)), DMA((8,)), DMA((8,)), DMA((WAVES,)),
        ],
        compiler_params=pltpu.CompilerParams(
            collective_id=0, has_side_effects=True, vmem_limit_bytes=60 << 20
        ),
        name="step",
    )(
        hot_request, cold_request, hot_pos, cold_pos, bottom, labels, w_out,
        hot_table, cold_table, w_first, w_second,
    )


def update_kernel(gradient, acc, table, new_table, new_acc):
    first = lax.broadcasted_iota(jnp.int32, (LANES, LANES), 0)
    second = lax.broadcasted_iota(jnp.int32, (LANES, LANES), 1)
    diagonal = first == second
    for block in range(table.shape[0] // LANES):
        rows = slice(block * LANES, (block + 1) * LANES)
        grad = gradient[rows, :].astype(jnp.float32)
        spread_acc = jnp.where(diagonal, acc[block : block + 1, :], 0.0)
        new = jnp.sum(grad * grad * (1.0 / LANES) + spread_acc, axis=1, keepdims=True)
        new_table[rows, :] = table[rows, :] - STEP_RATE * grad * lax.rsqrt(new)
        new_acc[block : block + 1, :] = jnp.sum(jnp.where(diagonal, new, 0.0), axis=0, keepdims=True)


def update(gradient, acc, table, name):
    block = 1024
    rows = pl.BlockSpec((block, LANES), lambda n: (n, 0))
    packed = pl.BlockSpec((block // LANES, LANES), lambda n: (n, 0))
    return pl.pallas_call(
        update_kernel,
        grid=(table.shape[0] // block,),
        out_shape=[
            jax.ShapeDtypeStruct(table.shape, jnp.float32),
            jax.ShapeDtypeStruct(acc.shape, jnp.float32),
        ],
        in_specs=[rows, packed, rows],
        out_specs=[rows, packed],
        name=name,
    )(gradient, acc, table)


def shards(
    hot_table, hot_acc, cold_table, cold_acc, bottom_out, labels,
    hot_owner, hot_offset, cold_owner, cold_offset, w_first, w_second, w_out,
):
    def by_lane(lookups):
        return jnp.transpose(lookups, (1, 2, 0)).reshape(-1, LANES)

    hot_request, hot_pos, cold_request, cold_pos = place_all(
        by_lane(hot_owner), by_lane(hot_offset), by_lane(cold_owner), by_lane(cold_offset)
    )
    hot_grad, cold_grad = train(
        hot_request, cold_request, hot_pos, cold_pos, bottom_out, labels.reshape(1, -1),
        w_out.reshape(1, -1), hot_table, cold_table, w_first, w_second,
    )
    new_hot, new_hot_acc = update(
        hot_grad.reshape(-1, LANES), hot_acc.reshape(-1, LANES), hot_table, "update_hot"
    )
    new_cold, new_cold_acc = update(cold_grad, cold_acc.reshape(-1, LANES), cold_table, "update_cold")
    return (new_hot, new_hot_acc.reshape(-1), new_cold, new_cold_acc.reshape(-1))


def solution(mesh):
    both = P(("group", "member"))
    in_specs = (P("member"), P("member")) + (both,) * 8 + (P(),) * 3
    out_specs = (P("member"), P("member"), both, both)
    return jax.shard_map(shards, mesh=mesh, in_specs=in_specs, out_specs=out_specs, check_vma=False)
```

time: 381 us -> 113 us (0.30)
  the two profiles are of different devices: /device:TPU:0 before, /device:TPU:1 now
where the time goes in v3:
time: 113 us; the launch traced here: 112 us
  Pallas kernels  105 us (93%)
  local copies, waits for them, and re-layouts  6.46 us (6%)
    pallas_call x1, Pallas kernels, train(): pl.pallas_call(step_kernel, out_shape=[jax.ShapeDtypeStruct((GROUPS, SLIC...  97.4 us
    pallas_call x2, Pallas kernels, update(): pl.pallas_call(update_kernel, grid=(table.shape[0] // block,), out_shape=...  7.01 us
    unnamed x16, local copies, waits for them, and re-layouts  5.17 us

profile of v3, /device:TPU:1, one launch (start us, length us, event | category | flops | bytes accessed | tf_op | source)
XLA Modules:
  0.0 112.4 jit_solution(5307869325563537471)
XLA Ops:
  0.6 0.0 copy-start.3
  0.6 0.7 copy-done.3
  1.3 0.0 copy-start.4
  1.3 0.7 copy-done.4
  2.0 0.0 copy-start.5
  2.0 0.7 copy-done.5
  2.7 0.0 copy-start.6
  2.7 0.7 copy-done.6
  3.4 0.9 place.1
  4.3 0.0 copy-start
  4.3 0.6 copy-done
  4.9 0.0 copy-start.1
  4.9 0.6 copy-done.1
  5.5 0.0 copy-start.2
  5.5 0.6 copy-done.2
  6.1 0.0 copy-start.7
  6.1 0.6 copy-done.7
  6.7 1.3 %reshape.46.w_out = bf16[1,2048]{1,0:T(2,128)(2,1)} reshape(bf16[2048]{0:T(1024)(128)(2,1)} %param.25) | data formatting | bytes 8192 | tf_op jit(solution)/shard_map/reshape | solution.py:508
  8.0 97.4 %step.1 = (bf16[8,256,128]{2,1,0:T(8,128)(2,1)}, f32[4096,128]{1,0:T(8,128)}) custom-call(s32[16,1,256]{2,1,0:T(1,128)} %copy-done.1, s32[128,1,128]{2,1,0:T(1,128)} %copy-done, s32[16,128]{1,0:T(8,128)} %copy-done.2, s32[8,128]{1,0:T(8,128)} %copy-done.7, bf16[128,128]{1,0:T(8,128)(2,1)} %bottom.1, f32[1,128]{1,0:T(1,128)} %bitcast.29, ...), custom_call_target="tpu_custom_call" | custom-call | tf_op jit(solution)/shard_map/step/pallas_call | solution.py:436
  105.4 4.6 %update_cold.1 = (f32[4096,128]{1,0:T(8,128)}, f32[32,128]{1,0:T(8,128)}) custom-call(f32[4096,128]{1,0:T(8,128)} %get-tuple-element.21.gradient, f32[32,128]{1,0:T(8,128)} %bitcast.27, f32[4096,128]{1,0:T(8,128)} %table.3), custom_call_target="tpu_custom_call" | custom-call | tf_op jit(solution)/shard_map/update_cold/pallas_call | solution.py:483
  110.0 2.4 %update_hot.1 = (f32[2048,128]{1,0:T(8,128)}, f32[16,128]{1,0:T(8,128)}) custom-call(bf16[2048,128]{1,0:T(8,128)(2,1)} %bitcast.26, f32[16,128]{1,0:T(8,128)} %bitcast.28, f32[2048,128]{1,0:T(8,128)} %table.2), custom_call_target="tpu_custom_call" | custom-call | tf_op jit(solution)/shard_map/update_hot/pallas_call | solution.py:483
Async XLA Ops:
  0.6 0.7 copy-start.3
  1.3 0.7 copy-start.4
  2.0 0.7 copy-start.5
  2.7 0.7 copy-start.6
  4.3 0.6 copy-start
  4.9 0.6 copy-start.1
  5.5 0.6 copy-start.2
  6.1 0.6 copy-start.7

commit v4 on v3

--- a/solution.py
+++ b/solution.py
@@ -22,7 +22,6 @@
 MESH = pl.DeviceIdType.MESH
 NT = (((1,), (1,)), ((), ()))
 
-VMEM = pl.BlockSpec(memory_space=pltpu.VMEM)
 ANY = pl.BlockSpec(memory_space=pl.ANY)
 DMA = pltpu.SemaphoreType.DMA
 
@@ -41,7 +40,7 @@
     )
 
 
-def place(owner_ref, offset_ref, owners, cap, request_ref, position_ref):
+def place(owner_ref, offset_ref, owners, cap, table_rows, request_ref, position_ref):
     rows = owner_ref.shape[0]
     owner_ids = lax.broadcasted_iota(jnp.int32, (owners, LANES), 0)
     hits = [(owner_ref[r : r + 1, :] == owner_ids).astype(jnp.float32) for r in range(rows)]
@@ -59,7 +58,9 @@
         count = counts[r * owners : (r + 1) * owners]
         slot = jnp.sum(hits[r] * (count[:, :LANES] + base), axis=0, keepdims=True).astype(jnp.int32)
         base = base + count[:, LANES:]
-        position_ref[r : r + 1, :] = owner_ref[r : r + 1, :] * cap + slot
+        position_ref[r : r + 1, :] = jnp.clip(
+            owner_ref[r : r + 1, :] * cap + slot, 0, owners * cap - 1
+        )
         offset = offset_ref[r : r + 1, :]
         high.append(hits[r] * (offset // 64).astype(jnp.float32))
         low.append(hits[r] * (offset % 64).astype(jnp.float32))
@@ -70,45 +71,28 @@
     placed = lax.dot_general(
         digits, jnp.concatenate(at_slot, axis=1), NT, preferred_element_type=jnp.float32
     )
-    requests = (placed[:owners] * 64.0 + placed[owners:]).astype(jnp.int32)
+    requests = jnp.clip(
+        (placed[:owners] * 64.0 + placed[owners:]).astype(jnp.int32), 0, table_rows - 1
+    )
     for owner in range(owners):
         request_ref[owner] = requests[owner : owner + 1, :]
 
 
-def place_kernel(
-    hot_owner, hot_offset, cold_owner, cold_offset, hot_request, hot_pos, cold_request, cold_pos
-):
-    place(hot_owner, hot_offset, MEMBERS, HCAP, hot_request, hot_pos)
-    place(cold_owner, cold_offset, DEVICES, CCAP, cold_request, cold_pos)
-
-
-def place_all(hot_owner, hot_offset, cold_owner, cold_offset):
-    shapes = [
-        (MEMBERS, 1, HCAP), (2 * TABLES, LANES), (DEVICES, 1, LANES), (TABLES, LANES)
-    ]
-    return pl.pallas_call(
-        place_kernel,
-        out_shape=[jax.ShapeDtypeStruct(shape, jnp.int32) for shape in shapes],
-        in_specs=[VMEM] * 4,
-        out_specs=[VMEM] * 4,
-        compiler_params=pltpu.CompilerParams(vmem_limit_bytes=32 << 20),
-        name="place",
-    )(hot_owner, hot_offset, cold_owner, cold_offset)
-
-
 WAVES = 8
 PAIRS = TABLES * LANES
 
 
 def step_kernel(
-    hot_request, cold_request, hot_pos, cold_pos, bottom, labels, w_out,
+    hot_owner_hbm, hot_offset_hbm, cold_owner_hbm, cold_offset_hbm, bottom_hbm, labels_hbm, out_hbm,
     hot_hbm, cold_hbm, first_hbm, second_hbm,
-    hot_grad, cold_grad,
+    hot_grad, cold_grad_hbm,
+    hot_owner, hot_offset, cold_owner, cold_offset, labels, w_out,
+    hot_request, cold_request, hot_pos, cold_pos, own_grad, cold_grad,
     hot_table, cold_table, w_first, w_second,
     hot_asked, cold_asked, hot_index, cold_index, hot_at, cold_at,
-    hot_out, cold_out, hot_rows, cold_rows, stage, hot_wide, cold_wide, features, pooled, terms,
+    hot_out, cold_out, hot_rows, cold_rows, stage, picked, hot_wide, cold_wide, features, pooled, terms,
     hot_send, cold_send, hot_got, cold_got, partial, part_out, part_got,
-    local_sem, send_sem, recv_sem, cold_sem,
+    local_sem, send_sem, recv_sem, cold_sem, present,
 ):
     group, member = lax.axis_index("group"), lax.axis_index("member")
     me = group * MEMBERS + member
@@ -133,25 +117,34 @@
         dz, dx = member_step(i)
         return lax.rem(z + 4 - dz, 4) * 4 + lax.rem(x + 4 - dx, 4)
 
+    def load(src, dst, n):
+        copy = pltpu.make_async_copy(src, dst, local_sem.at[n])
+        copy.start()
+        return copy
+
+    ids = [
+        load(hot_owner_hbm, hot_owner, 0), load(hot_offset_hbm, hot_offset, 1),
+        load(cold_owner_hbm, cold_owner, 2), load(cold_offset_hbm, cold_offset, 3),
+    ]
     barrier = pltpu.get_barrier_semaphore()
-    for k in range(GROUPS):
-        for d in range(MEMBERS):
-            if k or d:
-                pl.semaphore_signal(
-                    barrier, inc=1, device_id=(to_group[k], members[d]), device_id_type=MESH
-                )
-    loads = [
-        pltpu.make_async_copy(src, dst, local_sem.at[n])
-        for n, (src, dst) in enumerate(
-            [
-                (hot_hbm, hot_table), (cold_hbm, cold_table), (first_hbm, w_first),
-                (second_hbm, w_second), (hot_pos, hot_at), (cold_pos, cold_at),
-            ]
-        )
+    for d in range(1, MEMBERS):
+        pl.semaphore_signal(barrier, inc=1, device_id=(group, members[d]), device_id_type=MESH)
+    for k in range(1, GROUPS):
+        pl.semaphore_signal(barrier, inc=1, device_id=(to_group[k], member), device_id_type=MESH)
+    load_hot = load(hot_hbm, hot_table, 4)
+    load_cold = load(cold_hbm, cold_table, 5)
+    small = [
+        load(bottom_hbm, features.at[:, pl.ds(0, LANES)], 6), load(labels_hbm, labels, 7),
+        load(out_hbm, w_out, 8),
     ]
-    for load in loads:
-        load.start()
-    pl.semaphore_wait(barrier, DEVICES - 1)
+    load_first = load(first_hbm, w_first, 9)
+    load_second = load(second_hbm, w_second, 10)
+    ids[0].wait()
+    ids[1].wait()
+    place(hot_owner, hot_offset, MEMBERS, HCAP, HOT_ROWS, hot_request, hot_pos)
+    pl.semaphore_wait(barrier, MEMBERS - 1 + GROUPS - 1)
+    for k in range(1, GROUPS):
+        pl.semaphore_signal(present, inc=1, device_id=(to_group[k], member), device_id_type=MESH)
 
     beside = (group, members[1])
 
@@ -167,6 +160,13 @@
         return unused
 
     lax.fori_loop(1, MEMBERS, ask_hot, 0)
+
+    hot_asked[0] = hot_request[member]
+    ids[2].wait()
+    ids[3].wait()
+    place(cold_owner, cold_offset, DEVICES, CCAP, COLD_ROWS, cold_request, cold_pos)
+    index_loads = [load(hot_pos, hot_at, 11), load(cold_pos, cold_at, 12)]
+    pl.semaphore_wait(present, GROUPS - 1)
 
     def ask_cold_at(i, groups):
         to = to_member(i)
@@ -182,13 +182,11 @@
 
     ask_cold_at(0, range(1, GROUPS))
     lax.fori_loop(1, MEMBERS, ask_cold, 0)
-    hot_asked[0] = hot_request[member]
     cold_asked[0] = cold_request[me]
 
     drain(hot_asked, 1, MEMBERS - 1, send_sem.at[0], recv_sem.at[0]).wait_recv()
-    to_scalars = pltpu.make_async_copy(hot_asked, hot_index, local_sem.at[6])
-    to_scalars.start()
-    loads[0].wait()
+    to_scalars = load(hot_asked, hot_index, 13)
+    load_hot.wait()
     to_scalars.wait()
 
     def pick(table, index, row, first, target):
@@ -216,9 +214,8 @@
     serve_hot(0, hot_rows.at[member])
 
     drain(cold_asked, 1, DEVICES - 1, send_sem.at[1], recv_sem.at[1]).wait_recv()
-    to_scalars = pltpu.make_async_copy(cold_asked, cold_index, local_sem.at[7])
-    to_scalars.start()
-    loads[1].wait()
+    to_scalars = load(cold_asked, cold_index, 14)
+    load_cold.wait()
     to_scalars.wait()
 
     def serve_cold_at(i, groups):
@@ -239,36 +236,45 @@
     lax.fori_loop(1, MEMBERS, serve_cold, 0)
     pick(cold_table, cold_index, 0, 0, cold_rows.at[me])
 
-    loads[4].wait()
-    loads[5].wait()
+    for copy in index_loads + small:
+        copy.wait()
+    unroll = 16
     drain(hot_rows, 0, MEMBERS - 1, send_sem.at[2], recv_sem.at[2]).wait_recv()
     hot_wide[...] = hot_rows[...].astype(jnp.float32).reshape(hot_wide.shape)
-    features[:, :LANES] = bottom[...]
-    drain(cold_rows, 0, DEVICES - 1, send_sem.at[3], recv_sem.at[3]).wait_recv()
-    cold_wide[...] = cold_rows[...].astype(jnp.float32).reshape(cold_wide.shape)
-    unroll = 16
     for table in range(TABLES):
 
-        def combine(k, unused):
+        def combine_hot(k, unused):
             for j in range(unroll):
                 b = k * unroll + j
-                hot = (
+                pooled[table, pl.ds(b, 1), :] = (
                     hot_wide[pl.ds(hot_at[2 * table, b], 1), :]
                     + hot_wide[pl.ds(hot_at[2 * table + 1, b], 1), :]
                 )
-                pooled[table, pl.ds(b, 1), :] = hot + cold_wide[pl.ds(cold_at[table, b], 1), :]
             return unused
 
-        lax.fori_loop(0, LANES // unroll, combine, 0)
-        features[:, (table + 1) * LANES : (table + 2) * LANES] = pooled[table].astype(jnp.bfloat16)
-
-    loads[2].wait()
+        lax.fori_loop(0, LANES // unroll, combine_hot, 0)
+    drain(cold_rows, 0, DEVICES - 1, send_sem.at[3], recv_sem.at[3]).wait_recv()
+    cold_wide[...] = cold_rows[...].astype(jnp.float32).reshape(cold_wide.shape)
+    for table in range(TABLES):
+
+        def combine_cold(k, unused):
+            for j in range(unroll):
+                b = k * unroll + j
+                picked[pl.ds(b, 1), :] = cold_wide[pl.ds(cold_at[table, b], 1), :]
+            return unused
+
+        lax.fori_loop(0, LANES // unroll, combine_cold, 0)
+        features[:, (table + 1) * LANES : (table + 2) * LANES] = (
+            pooled[table] + picked[...]
+        ).astype(jnp.bfloat16)
+
+    load_first.wait()
     first_pre = jnp.dot(features[...], w_first[...], preferred_element_type=jnp.float32)
     first_act = jnp.maximum(first_pre, 0.0).astype(jnp.bfloat16)
-    loads[3].wait()
+    load_second.wait()
     second_pre = jnp.dot(first_act, w_second[...], preferred_element_type=jnp.float32)
     second_act = jnp.maximum(second_pre, 0.0).astype(jnp.bfloat16)
-    out_wide = w_out[...].astype(jnp.float32)
+    out_wide = w_out[...].astype(jnp.float32).reshape(1, -1)
     score = jnp.sum(second_act.astype(jnp.float32) * out_wide, axis=1, keepdims=True)
     row_id = lax.broadcasted_iota(jnp.int32, (LANES, LANES), 0)
     lane_id = lax.broadcasted_iota(jnp.int32, (LANES, LANES), 1)
@@ -323,7 +329,6 @@
         wanted = [cold_pos[table : table + 1, :] for table in range(TABLES)]
         sent = jnp.dot(one_hot(rows, wanted), terms[...], preferred_element_type=jnp.float32)
         cold_send[i] = sent.astype(jnp.bfloat16).reshape(GROUPS, CCAP, LANES)
-        return to
 
     def send_cold(i, to, groups):
         wave = lax.div(i, MEMBERS // WAVES)
@@ -333,13 +338,16 @@
                 (to_group[k], to),
             ).start()
 
-    def spread_cold_send(i, unused):
-        send_cold(i, spread_cold(i), range(GROUPS))
-        return unused
-
-    send_cold(0, spread_cold(0), range(1, GROUPS))
+    def spread_only(i, unused):
+        spread_cold(i)
+        return unused
+
+    def send_only(i, unused):
+        send_cold(i, to_member(i), range(GROUPS))
+        return unused
+
+    lax.fori_loop(0, MEMBERS, spread_only, 0)
     cold_got[0] = cold_send[0, 0]
-    lax.fori_loop(1, half, spread_cold_send, 0)
 
     def add_hot(first, steps, total):
         for i in steps:
@@ -351,13 +359,15 @@
         return total
 
     drain(hot_got, 1, half - 1, send_sem.at[4], recv_sem.at[4]).wait_recv()
+    send_cold(0, member, range(1, GROUPS))
+    lax.fori_loop(1, half, send_only, 0)
 
     def early(block, unused):
         partial[block] = add_hot(block * SLICE, range(half), jnp.zeros((SLICE, LANES), jnp.float32))
         return unused
 
     lax.fori_loop(0, GROUPS, early, 0)
-    lax.fori_loop(half, MEMBERS, spread_cold_send, 0)
+    lax.fori_loop(half, MEMBERS, send_only, 0)
     drain(hot_got, half, MEMBERS - half, send_sem.at[4], recv_sem.at[5]).wait_recv()
     for k in list(range(1, GROUPS)) + [0]:
         to = to_group[k]
@@ -403,19 +413,23 @@
 
     drain(cold_got, 1, per_wave - 1, send_sem.at[5], cold_sem.at[0]).wait_recv()
     settle_cold(0, True)
-    lax.fori_loop(1, 4, cold_wave, 0)
+    lax.fori_loop(1, 3, cold_wave, 0)
 
     drain(part_got, 1, GROUPS - 1, send_sem.at[6], recv_sem.at[6]).wait_recv()
     total = partial[0]
     for k in range(1, GROUPS):
         total = total + part_got[k].astype(jnp.float32)
-    hot_grad[group] = total.astype(jnp.bfloat16)
+    own_grad[...] = total.astype(jnp.bfloat16)
+    keep_own = load(own_grad, hot_grad.at[group], 15)
     for k in range(1, GROUPS):
         remote(
-            hot_grad.at[group], hot_grad.at[group], send_sem.at[7], recv_sem.at[7],
+            own_grad, hot_grad.at[group], send_sem.at[7], recv_sem.at[7],
             (to_group[k], member),
         ).start()
-    lax.fori_loop(4, WAVES, cold_wave, 0)
+    lax.fori_loop(3, WAVES, cold_wave, 0)
+    keep_cold = load(cold_grad, cold_grad_hbm, 16)
+    keep_own.wait()
+    keep_cold.wait()
 
     drain(hot_asked, 1, MEMBERS - 1, send_sem.at[0], recv_sem.at[0]).wait_send()
     drain(cold_asked, 1, DEVICES - 1, send_sem.at[1], recv_sem.at[1]).wait_send()
@@ -428,7 +442,7 @@
 
 
 def train(
-    hot_request, cold_request, hot_pos, cold_pos, bottom, labels, w_out,
+    hot_owner, hot_offset, cold_owner, cold_offset, bottom, labels, w_out,
     hot_table, cold_table, w_first, w_second,
 ):
     i32 = jnp.int32
@@ -439,58 +453,97 @@
             jax.ShapeDtypeStruct((GROUPS, SLICE, LANES), jnp.bfloat16),
             jax.ShapeDtypeStruct((COLD_ROWS, LANES), jnp.float32),
         ],
-        in_specs=[VMEM] * 7 + [ANY] * 4,
-        out_specs=[VMEM] * 2,
+        in_specs=[ANY] * 11,
+        out_specs=[ANY] * 2,
         scratch_shapes=[
+            pltpu.VMEM((2 * TABLES, LANES), i32), pltpu.VMEM((2 * TABLES, LANES), i32),
+            pltpu.VMEM((TABLES, LANES), i32), pltpu.VMEM((TABLES, LANES), i32),
+            f32(1, LANES), b16(*w_out.shape),
+            pltpu.VMEM((MEMBERS, 1, HCAP), i32), pltpu.VMEM((DEVICES, 1, LANES), i32),
+            pltpu.VMEM((2 * TABLES, LANES), i32), pltpu.VMEM((TABLES, LANES), i32),
+            b16(SLICE, LANES), f32(COLD_ROWS, LANES),
             f32(HOT_ROWS, LANES), f32(COLD_ROWS, LANES), b16(*w_first.shape), b16(*w_second.shape),
             pltpu.VMEM((MEMBERS, 1, HCAP), i32), pltpu.VMEM((DEVICES, 1, LANES), i32),
             pltpu.SMEM((MEMBERS, 1, HCAP), i32), pltpu.SMEM((DEVICES, 1, LANES), i32),
             pltpu.SMEM((2 * TABLES, LANES), i32), pltpu.SMEM((TABLES, LANES), i32),
             b16(*hot_block), b16(*cold_block), b16(*hot_block), b16(*cold_block), f32(CCAP, LANES),
-            f32(MEMBERS * HCAP, LANES), f32(DEVICES * CCAP, LANES),
+            f32(LANES, LANES), f32(MEMBERS * HCAP, LANES), f32(DEVICES * CCAP, LANES),
             b16(LANES, w_first.shape[0]), f32(TABLES, LANES, LANES), b16(PAIRS, LANES),
             b16(*hot_block), b16(MEMBERS, GROUPS, CCAP, LANES), b16(*hot_block), b16(*cold_block),
             f32(GROUPS, SLICE, LANES), b16(GROUPS, SLICE, LANES), b16(GROUPS, SLICE, LANES),
-            DMA((8,)), DMA((8,)), DMA((8,)), DMA((WAVES,)),
+            DMA((17,)), DMA((8,)), DMA((8,)), DMA((WAVES,)), pltpu.SemaphoreType.REGULAR,
         ],
         compiler_params=pltpu.CompilerParams(
-            collective_id=0, has_side_effects=True, vmem_limit_bytes=60 << 20
+            collective_id=0, has_side_effects=True, vmem_limit_bytes=62 << 20
         ),
         name="step",
     )(
-        hot_request, cold_request, hot_pos, cold_pos, bottom, labels, w_out,
+        hot_owner, hot_offset, cold_owner, cold_offset, bottom, labels, w_out,
         hot_table, cold_table, w_first, w_second,
     )
 
 
-def update_kernel(gradient, acc, table, new_table, new_acc):
+def split(value, parts):
+    found = []
+    for _ in range(parts):
+        part = value.astype(jnp.bfloat16)
+        found.append(part)
+        value = value - part.astype(jnp.float32)
+    return found
+
+
+def update_kernel(
+    hot_grad, hot_acc, hot_table, cold_grad, cold_acc, cold_table,
+    new_hot, new_hot_acc, new_cold, new_cold_acc,
+):
     first = lax.broadcasted_iota(jnp.int32, (LANES, LANES), 0)
     second = lax.broadcasted_iota(jnp.int32, (LANES, LANES), 1)
     diagonal = first == second
-    for block in range(table.shape[0] // LANES):
-        rows = slice(block * LANES, (block + 1) * LANES)
-        grad = gradient[rows, :].astype(jnp.float32)
-        spread_acc = jnp.where(diagonal, acc[block : block + 1, :], 0.0)
-        new = jnp.sum(grad * grad * (1.0 / LANES) + spread_acc, axis=1, keepdims=True)
-        new_table[rows, :] = table[rows, :] - STEP_RATE * grad * lax.rsqrt(new)
-        new_acc[block : block + 1, :] = jnp.sum(jnp.where(diagonal, new, 0.0), axis=0, keepdims=True)
-
-
-def update(gradient, acc, table, name):
-    block = 1024
-    rows = pl.BlockSpec((block, LANES), lambda n: (n, 0))
-    packed = pl.BlockSpec((block // LANES, LANES), lambda n: (n, 0))
+    weights = jnp.concatenate(
+        [jnp.full((2 * LANES, LANES), 1.0 / LANES), jnp.ones((3 * LANES, LANES))], axis=0
+    ).astype(jnp.bfloat16)
+
+    def adagrad(gradient, acc, table, new_table, new_acc):
+        for block in range(table.shape[0] // LANES):
+            rows = slice(block * LANES, (block + 1) * LANES)
+            grad = gradient[rows, :].astype(jnp.float32)
+            spread_acc = jnp.where(diagonal, acc[0, block : block + 1, :], 0.0)
+            parts = jnp.concatenate(split(grad * grad, 2) + split(spread_acc, 3), axis=1)
+            new = jnp.dot(parts, weights, preferred_element_type=jnp.float32)
+            new_table[rows, :] = table[rows, :] - STEP_RATE * grad * lax.rsqrt(new)
+            new_acc[0, block : block + 1, :] = jnp.sum(
+                jnp.where(diagonal, new, 0.0), axis=0, keepdims=True
+            )
+
+    adagrad(hot_grad, hot_acc, hot_table, new_hot, new_hot_acc)
+    adagrad(cold_grad, cold_acc, cold_table, new_cold, new_cold_acc)
+
+
+def update(hot_grad, hot_acc, hot_table, cold_grad, cold_acc, cold_table):
+    steps = 4
+    in_specs, out_specs, out_shape = [], [], []
+    for table in (hot_table, cold_table):
+        block = table.shape[0] // steps
+        rows = pl.BlockSpec((block, LANES), lambda n: (n, 0))
+        packed = pl.BlockSpec((1, block // LANES, LANES), lambda n: (n, 0, 0))
+        in_specs += [rows, packed, rows]
+        out_specs += [rows, packed]
+        out_shape += [
+            jax.ShapeDtypeStruct(table.shape, jnp.float32),
+            jax.ShapeDtypeStruct((steps, block // LANES, LANES), jnp.float32),
+        ]
     return pl.pallas_call(
         update_kernel,
-        grid=(table.shape[0] // block,),
-        out_shape=[
-            jax.ShapeDtypeStruct(table.shape, jnp.float32),
-            jax.ShapeDtypeStruct(acc.shape, jnp.float32),
-        ],
-        in_specs=[rows, packed, rows],
-        out_specs=[rows, packed],
-        name=name,
-    )(gradient, acc, table)
+        grid=(steps,),
+        out_shape=out_shape,
+        in_specs=in_specs,
+        out_specs=out_specs,
+        compiler_params=pltpu.CompilerParams(vmem_limit_bytes=62 << 20),
+        name="update",
+    )(
+        hot_grad, hot_acc.reshape(steps, -1, LANES), hot_table,
+        cold_grad, cold_acc.reshape(steps, -1, LANES), cold_table,
+    )
 
 
 def shards(
@@ -500,17 +553,13 @@
     def by_lane(lookups):
         return jnp.transpose(lookups, (1, 2, 0)).reshape(-1, LANES)
 
-    hot_request, hot_pos, cold_request, cold_pos = place_all(
-        by_lane(hot_owner), by_lane(hot_offset), by_lane(cold_owner), by_lane(cold_offset)
-    )
     hot_grad, cold_grad = train(
-        hot_request, cold_request, hot_pos, cold_pos, bottom_out, labels.reshape(1, -1),
-        w_out.reshape(1, -1), hot_table, cold_table, w_first, w_second,
-    )
-    new_hot, new_hot_acc = update(
-        hot_grad.reshape(-1, LANES), hot_acc.reshape(-1, LANES), hot_table, "update_hot"
-    )
-    new_cold, new_cold_acc = update(cold_grad, cold_acc.reshape(-1, LANES), cold_table, "update_cold")
+        by_lane(hot_owner), by_lane(hot_offset), by_lane(cold_owner), by_lane(cold_offset),
+        bottom_out, labels.reshape(1, -1), w_out, hot_table, cold_table, w_first, w_second,
+    )
+    new_hot, new_hot_acc, new_cold, new_cold_acc = update(
+        hot_grad.reshape(-1, LANES), hot_acc, hot_table, cold_grad, cold_acc, cold_table
+    )
     return (new_hot, new_hot_acc.reshape(-1), new_cold, new_cold_acc.reshape(-1))
 
 

time: 113 us -> 101 us (0.89)
  local copies, waits for them, and re-layouts: 6.46 us -> 0 us
  Pallas kernels: 105 us -> 100 us
    unnamed x16 -> x0, local copies, waits for them, and re-layouts: 5.17 us -> none
    pallas_call x1, Pallas kernels: 97.4 us -> 94.4 us  [train(): pl.pallas_call(step_kernel, out_shape=[jax.ShapeDtypeStruct((GROUPS, SLIC...]
    pallas_call x3 -> x1, Pallas kernels: 7.88 us -> 6.05 us  [update(): pl.pallas_call(update_kernel, grid=(steps,), out_shape=out_shape, in_spec...]
    reshape x1 -> x0, local copies, waits for them, and re-layouts: 1.29 us -> none  [shards(): w_out.reshape(1, -1)]
where the time goes in v4:
time: 101 us
  Pallas kernels  100 us (99%)
    pallas_call x1, Pallas kernels, train(): pl.pallas_call(step_kernel, out_shape=[jax.ShapeDtypeStruct((GROUPS, SLIC...  94.4 us
    pallas_call x1, Pallas kernels, update(): pl.pallas_call(update_kernel, grid=(steps,), out_shape=out_shape, in_spec...  6.05 us

profile of v4, /device:TPU:1, one launch (start us, length us, event | category | flops | bytes accessed | tf_op | source)
XLA Modules:
  0.0 101.1 jit_solution(4789224059976751215)
XLA Ops:
  0.6 94.4 %step.1 = (bf16[8,256,128]{2,1,0:T(8,128)(2,1)}, f32[4096,128]{1,0:T(8,128)}) custom-call(s32[16,128]{1,0:T(8,128)} %bitcast.24, s32[16,128]{1,0:T(8,128)} %bitcast.25, s32[8,128]{1,0:T(8,128)} %bitcast.27, s32[8,128]{1,0:T(8,128)} %bitcast.28, bf16[128,128]{1,0:T(8,128)(2,1)} %bottom_hbm.1, f32[1,128]{1,0:T(1,128)} %bitcast.29, bf16[2048]{0:T(1024)(128)(2,1)} %out_hbm.1, ...), custom_call_target="tpu_custom_call" | custom-call | tf_op jit(solution)/shard_map/step/pallas_call | solution.py:450
  95.1 6.1 %update.1 = (f32[2048,128]{1,0:T(8,128)}, f32[4,4,128]{2,1,0:T(4,128)}, f32[4096,128]{1,0:T(8,128)}, f32[4,8,128]{2,1,0:T(8,128)}) custom-call(bf16[2048,128]{1,0:T(8,128)(2,1)} %bitcast.22, f32[4,4,128]{2,1,0:T(4,128)} %bitcast.26, f32[2048,128]{1,0:T(8,128)} %hot_table.1, f32[4096,128]{1,0:T(8,128)} %get-tuple-element.11.cold_grad, f32[4,8,128]{2,1,0:T(8,128)} %bitcast.23, ...), custom_call_target="tpu_custom_call" | custom-call | tf_op jit(solution)/shard_map/update/pallas_call | solution.py:535

commit v5 on v4

--- a/solution.py
+++ b/solution.py
@@ -79,6 +79,9 @@
 
 
 WAVES = 8
+CLASSES = 4
+HOT_CLASS = HOT_ROWS // CLASSES
+COLD_CLASS = COLD_ROWS // CLASSES
 PAIRS = TABLES * LANES
 
 
@@ -89,9 +92,10 @@
     hot_owner, hot_offset, cold_owner, cold_offset, labels, w_out,
     hot_request, cold_request, hot_pos, cold_pos, own_grad, cold_grad,
     hot_table, cold_table, w_first, w_second,
-    hot_asked, cold_asked, hot_index, cold_index, hot_at, cold_at,
+    hot_asked, cold_asked, cold_asked_mid, hot_index, cold_index, hot_at, cold_at,
     hot_out, cold_out, hot_rows, cold_rows, stage, picked, hot_wide, cold_wide, features, pooled, terms,
-    hot_send, cold_send, hot_got, cold_got, partial, part_out, part_got,
+    hot_send, cold_send, cold_mid, hot_got, cold_got, partial, part_out, part_got,
+    hot_ids, cold_ids, hot_mask, cold_mask, wide_values,
     local_sem, send_sem, recv_sem, cold_sem, present,
 ):
     group, member = lax.axis_index("group"), lax.axis_index("member")
@@ -160,29 +164,17 @@
         return unused
 
     lax.fori_loop(1, MEMBERS, ask_hot, 0)
-
     hot_asked[0] = hot_request[member]
     ids[2].wait()
     ids[3].wait()
     place(cold_owner, cold_offset, DEVICES, CCAP, COLD_ROWS, cold_request, cold_pos)
     index_loads = [load(hot_pos, hot_at, 11), load(cold_pos, cold_at, 12)]
-    pl.semaphore_wait(present, GROUPS - 1)
-
-    def ask_cold_at(i, groups):
-        to = to_member(i)
-        for k in groups:
-            remote(
-                cold_request.at[to_group[k] * MEMBERS + to], cold_asked.at[i * GROUPS + k],
-                send_sem.at[1], recv_sem.at[1], (to_group[k], to),
-            ).start()
-
-    def ask_cold(i, unused):
-        ask_cold_at(i, range(GROUPS))
-        return unused
-
-    ask_cold_at(0, range(1, GROUPS))
-    lax.fori_loop(1, MEMBERS, ask_cold, 0)
-    cold_asked[0] = cold_request[me]
+    for k in range(1, GROUPS):
+        remote(
+            cold_request.at[pl.ds(to_group[k] * MEMBERS, MEMBERS)], cold_asked_mid.at[:, k],
+            send_sem.at[1], recv_sem.at[1], (to_group[k], member),
+        ).start()
+    cold_asked_mid[:, 0] = cold_request[pl.ds(group * MEMBERS, MEMBERS)]
 
     drain(hot_asked, 1, MEMBERS - 1, send_sem.at[0], recv_sem.at[0]).wait_recv()
     to_scalars = load(hot_asked, hot_index, 13)
@@ -210,13 +202,26 @@
         ).start()
         return unused
 
-    lax.fori_loop(1, MEMBERS, serve_hot_send, 0)
+    def ask_cold(i, unused):
+        to = to_member(i)
+        remote(
+            cold_asked_mid.at[to], cold_asked.at[pl.ds(i * GROUPS, GROUPS)],
+            send_sem.at[8], recv_sem.at[8], (group, to),
+        ).start()
+        return unused
+
+    lax.fori_loop(1, 5, serve_hot_send, 0)
+    drain(cold_asked, 0, DEVICES - MEMBERS, send_sem.at[1], recv_sem.at[1]).wait_recv()
+    lax.fori_loop(1, MEMBERS, ask_cold, 0)
+    cold_asked[pl.ds(0, GROUPS)] = cold_asked_mid[member]
+    lax.fori_loop(5, MEMBERS, serve_hot_send, 0)
     serve_hot(0, hot_rows.at[member])
 
-    drain(cold_asked, 1, DEVICES - 1, send_sem.at[1], recv_sem.at[1]).wait_recv()
+    drain(cold_asked, 0, DEVICES - GROUPS, send_sem.at[8], recv_sem.at[8]).wait_recv()
     to_scalars = load(cold_asked, cold_index, 14)
     load_cold.wait()
     to_scalars.wait()
+    pl.semaphore_wait(present, GROUPS - 1)
 
     def serve_cold_at(i, groups):
         to = from_member(i)
@@ -253,6 +258,37 @@
             return unused
 
         lax.fori_loop(0, LANES // unroll, combine_hot, 0)
+    row_id = lax.broadcasted_iota(jnp.int32, (LANES, LANES), 0)
+    lane_id = lax.broadcasted_iota(jnp.int32, (LANES, LANES), 1)
+    diagonal = row_id == lane_id
+    ones = jnp.ones((LANES, LANES), jnp.bfloat16)
+    quarter = lax.div(lax.broadcasted_iota(jnp.int32, (1, LANES), 1), CCAP)
+
+    def note(asked, size, n, ids, mask):
+        ids[n] = lax.rem(asked, size)
+        which = lax.div(asked, size).astype(jnp.float32)
+        wide = jnp.dot(
+            jnp.where(diagonal, which, 0.0).astype(jnp.bfloat16), ones,
+            preferred_element_type=jnp.float32,
+        )
+        for q in range(CLASSES):
+            mask[q, n] = jnp.where(wide == q, 1.0, 0.0).astype(jnp.bfloat16)
+
+    def note_hot(i, unused):
+        for c in range(HCAP // LANES):
+            asked = hot_asked[i][:, c * LANES : (c + 1) * LANES]
+            note(asked, HOT_CLASS, i * (HCAP // LANES) + c, hot_ids, hot_mask)
+        return unused
+
+    def note_cold(n, unused):
+        asked = cold_asked[4 * n]
+        for q in range(1, 4):
+            asked = jnp.where(quarter == q, cold_asked[4 * n + q], asked)
+        note(asked, COLD_CLASS, n, cold_ids, cold_mask)
+        return unused
+
+    lax.fori_loop(0, MEMBERS, note_hot, 0)
+    lax.fori_loop(0, DEVICES // 4, note_cold, 0)
     drain(cold_rows, 0, DEVICES - 1, send_sem.at[3], recv_sem.at[3]).wait_recv()
     cold_wide[...] = cold_rows[...].astype(jnp.float32).reshape(cold_wide.shape)
     for table in range(TABLES):
@@ -276,9 +312,7 @@
     second_act = jnp.maximum(second_pre, 0.0).astype(jnp.bfloat16)
     out_wide = w_out[...].astype(jnp.float32).reshape(1, -1)
     score = jnp.sum(second_act.astype(jnp.float32) * out_wide, axis=1, keepdims=True)
-    row_id = lax.broadcasted_iota(jnp.int32, (LANES, LANES), 0)
-    lane_id = lax.broadcasted_iota(jnp.int32, (LANES, LANES), 1)
-    label = jnp.sum(jnp.where(row_id == lane_id, labels[...], 0.0), axis=1, keepdims=True)
+    label = jnp.sum(jnp.where(diagonal, labels[...], 0.0), axis=1, keepdims=True)
     delta = jax.nn.sigmoid(score) - label
     grad_second = jnp.where(second_pre > 0, delta * out_wide, 0.0).astype(jnp.bfloat16)
     back_second = lax.dot_general(grad_second, w_second[...], NT, preferred_element_type=jnp.float32)
@@ -305,139 +339,170 @@
             one_hot(slot_id, wanted), terms[...], preferred_element_type=jnp.float32
         ).astype(jnp.bfloat16)
 
-    def spread_hot_send(wave):
-        def send(i, unused):
-            to = to_member(i)
-            hot_send[i] = spread_hot(to)
+    half = MEMBERS // 2
+
+    def spread_hot_send(i):
+        to = members[i * 7 % MEMBERS]
+        hot_send[i] = spread_hot(to)
+        remote(
+            hot_send.at[i], hot_got.at[i], send_sem.at[4], recv_sem.at[4 + i // half], (group, to)
+        ).start()
+
+    cold_wanted = [cold_pos[table : table + 1, :] for table in range(TABLES)]
+    piece = MEMBERS // 2
+
+    def spread_cold(k, target):
+        for first in range(0, MEMBERS, piece):
+            rows = jnp.concatenate(
+                [
+                    slot_id[:CCAP] + (to_group[k] * MEMBERS + members[i * 7 % MEMBERS]) * CCAP
+                    for i in range(first, first + piece)
+                ],
+                axis=0,
+            )
+            sent = jnp.dot(
+                one_hot(rows, cold_wanted), terms[...], preferred_element_type=jnp.float32
+            )
+            target[pl.ds(first, piece)] = sent.astype(jnp.bfloat16).reshape(piece, CCAP, LANES)
+
+    for k in range(1, GROUPS):
+        spread_hot_send(2 * k - 1)
+        spread_hot_send(2 * k)
+        spread_cold(k, cold_send.at[k])
+        remote(
+            cold_send.at[k], cold_mid.at[:, k], send_sem.at[5], recv_sem.at[9],
+            (to_group[k], member),
+        ).start()
+    spread_hot_send(MEMBERS - 1)
+    hot_got[0] = spread_hot(member)
+    spread_cold(0, cold_mid.at[:, 0])
+
+    def pass_cold(i, unused):
+        to = to_member(i)
+        remote(
+            cold_mid.at[i], cold_got.at[pl.ds(i * GROUPS, GROUPS)], send_sem.at[9],
+            cold_sem.at[lax.div(i, MEMBERS // WAVES)], (group, to),
+        ).start()
+        return unused
+
+    def wide_sums(rows, ids, first, count, values):
+        chosen = one_hot(rows, [ids[first + c] for c in range(count)])
+        return jnp.dot(chosen, values[: count * LANES, :], preferred_element_type=jnp.float32)
+
+    def widen(got, mask, first, count):
+        for c in range(count):
+            for q in range(CLASSES):
+                wide_values[c * LANES : (c + 1) * LANES, q * LANES : (q + 1) * LANES] = (
+                    got(c) * mask[q, first + c]
+                )
+
+    per_source = HCAP // LANES
+    half_blocks = half * per_source
+
+    def hot_part(first):
+        def got(c):
+            i, part = (first + c) // per_source, (first + c) % per_source
+            return hot_got[i, part * LANES : (part + 1) * LANES, :]
+
+        widen(got, hot_mask, first, half_blocks)
+
+    def hot_rows_of(h):
+        return jnp.concatenate(
+            [row_id + h * LANES, row_id + (SLICE + h * LANES)], axis=0
+        )
+
+    drain(hot_got, 1, half - 1, send_sem.at[4], recv_sem.at[4]).wait_recv()
+    hot_part(0)
+    for h in range(2):
+        sums = wide_sums(hot_rows_of(h), hot_ids, 0, half_blocks, wide_values)
+        for g in range(GROUPS):
+            partial[h, g] = sums[
+                g % 2 * LANES : (g % 2 + 1) * LANES, g // 2 * LANES : (g // 2 + 1) * LANES
+            ]
+    drain(cold_got, 0, DEVICES - MEMBERS, send_sem.at[5], recv_sem.at[9]).wait_recv()
+    lax.fori_loop(1, MEMBERS, pass_cold, 0)
+    cold_got[pl.ds(0, GROUPS)] = cold_mid[0]
+    drain(hot_got, half, MEMBERS - half, send_sem.at[4], recv_sem.at[5]).wait_recv()
+    hot_part(half_blocks)
+    for h in range(2):
+        sums = wide_sums(hot_rows_of(h), hot_ids, half_blocks, half_blocks, wide_values)
+        for g in range(GROUPS):
+            total = partial[h, g] + sums[
+                g % 2 * LANES : (g % 2 + 1) * LANES, g // 2 * LANES : (g // 2 + 1) * LANES
+            ]
+            partial[h, g] = total
+            part_out[h, g] = total.astype(jnp.bfloat16)
+        for k in range(1, GROUPS):
             remote(
-                hot_send.at[i], hot_got.at[i], send_sem.at[4], recv_sem.at[4 + wave], (group, to)
+                part_out.at[h, to_group[k]], part_got.at[h, k], send_sem.at[6], recv_sem.at[10 + h],
+                (to_group[k], member),
             ).start()
-            return unused
-
-        return send
-
-    half = MEMBERS // 2
-    lax.fori_loop(1, half, spread_hot_send(0), 0)
-    lax.fori_loop(half, MEMBERS, spread_hot_send(1), 0)
-    hot_got[0] = spread_hot(member)
-
-    def spread_cold(i):
-        to = to_member(i)
-        rows = jnp.concatenate(
-            [slot_id[:CCAP] + (to_group[k] * MEMBERS + to) * CCAP for k in range(GROUPS)], axis=0
-        )
-        wanted = [cold_pos[table : table + 1, :] for table in range(TABLES)]
-        sent = jnp.dot(one_hot(rows, wanted), terms[...], preferred_element_type=jnp.float32)
-        cold_send[i] = sent.astype(jnp.bfloat16).reshape(GROUPS, CCAP, LANES)
-
-    def send_cold(i, to, groups):
-        wave = lax.div(i, MEMBERS // WAVES)
-        for k in groups:
+
+    def share(h):
+        part = part_got.at[h, pl.ds(1, GROUPS - 1)]
+        remote(part, part, send_sem.at[6], recv_sem.at[10 + h], beside).wait_recv()
+        total = partial[h, group]
+        for k in range(1, GROUPS):
+            total = total + part_got[h, k].astype(jnp.float32)
+        own_grad[h] = total.astype(jnp.bfloat16)
+        for k in range(1, GROUPS):
             remote(
-                cold_send.at[i, k], cold_got.at[i * GROUPS + k], send_sem.at[5], cold_sem.at[wave],
-                (to_group[k], to),
+                own_grad.at[h], hot_grad.at[group, h], send_sem.at[7], recv_sem.at[7],
+                (to_group[k], member),
             ).start()
-
-    def spread_only(i, unused):
-        spread_cold(i)
-        return unused
-
-    def send_only(i, unused):
-        send_cold(i, to_member(i), range(GROUPS))
-        return unused
-
-    lax.fori_loop(0, MEMBERS, spread_only, 0)
-    cold_got[0] = cold_send[0, 0]
-
-    def add_hot(first, steps, total):
-        for i in steps:
-            asked = hot_asked[i] - first
-            wanted = [asked[:, c * LANES : (c + 1) * LANES] for c in range(HCAP // LANES)]
-            total = total + jnp.dot(
-                one_hot(slot_id, wanted), hot_got[i], preferred_element_type=jnp.float32
-            )
-        return total
-
-    drain(hot_got, 1, half - 1, send_sem.at[4], recv_sem.at[4]).wait_recv()
-    send_cold(0, member, range(1, GROUPS))
-    lax.fori_loop(1, half, send_only, 0)
-
-    def early(block, unused):
-        partial[block] = add_hot(block * SLICE, range(half), jnp.zeros((SLICE, LANES), jnp.float32))
-        return unused
-
-    lax.fori_loop(0, GROUPS, early, 0)
-    lax.fori_loop(half, MEMBERS, send_only, 0)
-    drain(hot_got, half, MEMBERS - half, send_sem.at[4], recv_sem.at[5]).wait_recv()
-    for k in list(range(1, GROUPS)) + [0]:
-        to = to_group[k]
-        total = add_hot(to * SLICE, range(half, MEMBERS), partial[to])
-        if k == 0:
-            own = total
-        else:
-            part_out[k] = total.astype(jnp.bfloat16)
-            remote(
-                part_out.at[k], part_got.at[k], send_sem.at[6], recv_sem.at[6], (to, member)
-            ).start()
-    partial[0] = own
 
     block_rows = 512
     per_wave = DEVICES // WAVES
+    wave_blocks = per_wave * CCAP // LANES
     big_id = lax.broadcasted_iota(jnp.int32, (block_rows, LANES), 0)
-    quarter = lax.div(lax.broadcasted_iota(jnp.int32, (1, LANES), 1), CCAP)
-
-    def settle_cold(wave, first_wave):
-        asked = []
-        for c in range(per_wave // 4):
-            row = cold_asked[wave * per_wave + 4 * c]
-            for q in range(1, 4):
-                row = jnp.where(quarter == q, cold_asked[wave * per_wave + 4 * c + q], row)
-            asked.append(row)
-        values = cold_got[pl.ds(wave * per_wave, per_wave)].reshape(per_wave * CCAP, LANES)
+
+    def settle_cold(wave, waves):
+        for n in range(wave, wave + waves):
+            skip = GROUPS if n == 0 else 0
+            drain(
+                cold_got, n * per_wave + skip, per_wave - skip, send_sem.at[9], cold_sem.at[n]
+            ).wait_recv()
+        first, count = wave * wave_blocks, waves * wave_blocks
+
+        def got(c):
+            at = (first + c) * LANES // CCAP
+            return cold_got[at : at + LANES // CCAP].reshape(LANES, LANES)
+
+        widen(got, cold_mask, first, count)
 
         def block(n, unused):
-            first = pl.multiple_of(n * block_rows, block_rows)
-            rows = pl.ds(first, block_rows)
-            sums = jnp.dot(
-                one_hot(big_id + first, asked), values, preferred_element_type=jnp.float32
-            )
-            cold_grad[rows, :] = sums if first_wave else cold_grad[rows, :] + sums
+            start = pl.multiple_of(n * block_rows, block_rows)
+            sums = wide_sums(big_id + start, cold_ids, first, count, wide_values)
+            for q in range(CLASSES):
+                rows = pl.ds(start + q * COLD_CLASS, block_rows)
+                part = sums[:, q * LANES : (q + 1) * LANES]
+                cold_grad[rows, :] = part if wave == 0 else cold_grad[rows, :] + part
             return unused
 
-        lax.fori_loop(0, COLD_ROWS // block_rows, block, 0)
-
-    def cold_wave(wave, unused):
-        drain(cold_got, wave * per_wave, per_wave, send_sem.at[5], cold_sem.at[wave]).wait_recv()
-        settle_cold(wave, False)
-        return unused
-
-    drain(cold_got, 1, per_wave - 1, send_sem.at[5], cold_sem.at[0]).wait_recv()
-    settle_cold(0, True)
-    lax.fori_loop(1, 3, cold_wave, 0)
-
-    drain(part_got, 1, GROUPS - 1, send_sem.at[6], recv_sem.at[6]).wait_recv()
-    total = partial[0]
-    for k in range(1, GROUPS):
-        total = total + part_got[k].astype(jnp.float32)
-    own_grad[...] = total.astype(jnp.bfloat16)
+        lax.fori_loop(0, COLD_CLASS // block_rows, block, 0)
+
+    settle_cold(0, 2)
+    share(0)
+    settle_cold(2, 2)
+    share(1)
     keep_own = load(own_grad, hot_grad.at[group], 15)
-    for k in range(1, GROUPS):
-        remote(
-            own_grad, hot_grad.at[group], send_sem.at[7], recv_sem.at[7],
-            (to_group[k], member),
-        ).start()
-    lax.fori_loop(3, WAVES, cold_wave, 0)
+    settle_cold(4, 2)
+    settle_cold(6, 1)
+    settle_cold(7, 1)
     keep_cold = load(cold_grad, cold_grad_hbm, 16)
     keep_own.wait()
     keep_cold.wait()
 
     drain(hot_asked, 1, MEMBERS - 1, send_sem.at[0], recv_sem.at[0]).wait_send()
-    drain(cold_asked, 1, DEVICES - 1, send_sem.at[1], recv_sem.at[1]).wait_send()
+    drain(cold_asked, 0, DEVICES - MEMBERS, send_sem.at[1], recv_sem.at[1]).wait_send()
+    drain(cold_asked, 0, DEVICES - GROUPS, send_sem.at[8], recv_sem.at[8]).wait_send()
     drain(hot_out, 1, MEMBERS - 1, send_sem.at[2], recv_sem.at[2]).wait_send()
     drain(cold_out, 1, DEVICES - 1, send_sem.at[3], recv_sem.at[3]).wait_send()
     drain(hot_send, 1, MEMBERS - 1, send_sem.at[4], recv_sem.at[4]).wait_send()
-    drain(cold_got, 1, DEVICES - 1, send_sem.at[5], recv_sem.at[4]).wait_send()
-    drain(part_out, 1, GROUPS - 1, send_sem.at[6], recv_sem.at[6]).wait_send()
+    drain(cold_got, 0, DEVICES - MEMBERS, send_sem.at[5], recv_sem.at[8]).wait_send()
+    drain(cold_got, 0, DEVICES - GROUPS, send_sem.at[9], recv_sem.at[8]).wait_send()
+    sent = part_out.at[:, pl.ds(1, GROUPS - 1)]
+    remote(sent, sent, send_sem.at[6], recv_sem.at[6], beside).wait_send()
     drain(hot_grad, 1, GROUPS - 1, send_sem.at[7], recv_sem.at[7]).wait()
 
 
@@ -450,7 +515,7 @@
     return pl.pallas_call(
         step_kernel,
         out_shape=[
-            jax.ShapeDtypeStruct((GROUPS, SLICE, LANES), jnp.bfloat16),
+            jax.ShapeDtypeStruct((GROUPS, 2, LANES, LANES), jnp.bfloat16),
             jax.ShapeDtypeStruct((COLD_ROWS, LANES), jnp.float32),
         ],
         in_specs=[ANY] * 11,
@@ -461,17 +526,23 @@
             f32(1, LANES), b16(*w_out.shape),
             pltpu.VMEM((MEMBERS, 1, HCAP), i32), pltpu.VMEM((DEVICES, 1, LANES), i32),
             pltpu.VMEM((2 * TABLES, LANES), i32), pltpu.VMEM((TABLES, LANES), i32),
-            b16(SLICE, LANES), f32(COLD_ROWS, LANES),
+            b16(2, LANES, LANES), f32(COLD_ROWS, LANES),
             f32(HOT_ROWS, LANES), f32(COLD_ROWS, LANES), b16(*w_first.shape), b16(*w_second.shape),
             pltpu.VMEM((MEMBERS, 1, HCAP), i32), pltpu.VMEM((DEVICES, 1, LANES), i32),
-            pltpu.SMEM((MEMBERS, 1, HCAP), i32), pltpu.SMEM((DEVICES, 1, LANES), i32),
+            pltpu.VMEM((MEMBERS, GROUPS, 1, LANES), i32), pltpu.SMEM((MEMBERS, 1, HCAP), i32), pltpu.SMEM((DEVICES, 1, LANES), i32),
             pltpu.SMEM((2 * TABLES, LANES), i32), pltpu.SMEM((TABLES, LANES), i32),
             b16(*hot_block), b16(*cold_block), b16(*hot_block), b16(*cold_block), f32(CCAP, LANES),
             f32(LANES, LANES), f32(MEMBERS * HCAP, LANES), f32(DEVICES * CCAP, LANES),
             b16(LANES, w_first.shape[0]), f32(TABLES, LANES, LANES), b16(PAIRS, LANES),
-            b16(*hot_block), b16(MEMBERS, GROUPS, CCAP, LANES), b16(*hot_block), b16(*cold_block),
-            f32(GROUPS, SLICE, LANES), b16(GROUPS, SLICE, LANES), b16(GROUPS, SLICE, LANES),
-            DMA((17,)), DMA((8,)), DMA((8,)), DMA((WAVES,)), pltpu.SemaphoreType.REGULAR,
+            b16(*hot_block), b16(GROUPS, MEMBERS, CCAP, LANES),
+            b16(MEMBERS, GROUPS, CCAP, LANES), b16(*hot_block), b16(*cold_block),
+            f32(2, GROUPS, LANES, LANES), b16(2, GROUPS, LANES, LANES), b16(2, GROUPS, LANES, LANES),
+            pltpu.VMEM((MEMBERS * HCAP // LANES, 1, LANES), i32),
+            pltpu.VMEM((DEVICES * CCAP // LANES, 1, LANES), i32),
+            b16(CLASSES, MEMBERS * HCAP // LANES, LANES, LANES),
+            b16(CLASSES, DEVICES * CCAP // LANES, LANES, LANES),
+            b16(MEMBERS * HCAP // 2, CLASSES * LANES),
+            DMA((17,)), DMA((10,)), DMA((12,)), DMA((WAVES,)), pltpu.SemaphoreType.REGULAR,
         ],
         compiler_params=pltpu.CompilerParams(
             collective_id=0, has_side_effects=True, vmem_limit_bytes=62 << 20
@@ -483,15 +554,6 @@
     )
 
 
-def split(value, parts):
-    found = []
-    for _ in range(parts):
-        part = value.astype(jnp.bfloat16)
-        found.append(part)
-        value = value - part.astype(jnp.float32)
-    return found
-
-
 def update_kernel(
     hot_grad, hot_acc, hot_table, cold_grad, cold_acc, cold_table,
     new_hot, new_hot_acc, new_cold, new_cold_acc,
@@ -499,17 +561,13 @@
     first = lax.broadcasted_iota(jnp.int32, (LANES, LANES), 0)
     second = lax.broadcasted_iota(jnp.int32, (LANES, LANES), 1)
     diagonal = first == second
-    weights = jnp.concatenate(
-        [jnp.full((2 * LANES, LANES), 1.0 / LANES), jnp.ones((3 * LANES, LANES))], axis=0
-    ).astype(jnp.bfloat16)
 
     def adagrad(gradient, acc, table, new_table, new_acc):
         for block in range(table.shape[0] // LANES):
             rows = slice(block * LANES, (block + 1) * LANES)
             grad = gradient[rows, :].astype(jnp.float32)
             spread_acc = jnp.where(diagonal, acc[0, block : block + 1, :], 0.0)
-            parts = jnp.concatenate(split(grad * grad, 2) + split(spread_acc, 3), axis=1)
-            new = jnp.dot(parts, weights, preferred_element_type=jnp.float32)
+            new = jnp.sum(grad * grad * (1.0 / LANES) + spread_acc, axis=1, keepdims=True)
             new_table[rows, :] = table[rows, :] - STEP_RATE * grad * lax.rsqrt(new)
             new_acc[0, block : block + 1, :] = jnp.sum(
                 jnp.where(diagonal, new, 0.0), axis=0, keepdims=True
@@ -520,7 +578,7 @@
 
 
 def update(hot_grad, hot_acc, hot_table, cold_grad, cold_acc, cold_table):
-    steps = 4
+    steps = 2
     in_specs, out_specs, out_shape = [], [], []
     for table in (hot_table, cold_table):
         block = table.shape[0] // steps

time: 101 us -> 97.9 us (0.969); the launches traced: 101 us -> 97 us
  Pallas kernels: 100 us -> 96.3 us
    pallas_call x1, Pallas kernels: 94.4 us -> 91.9 us  [train(): pl.pallas_call(step_kernel, out_shape=[jax.ShapeDtypeStruct((GROUPS, 2, L...]
    pallas_call x1, Pallas kernels: 6.05 us -> 4.35 us  [update(): pl.pallas_call(update_kernel, grid=(steps,), out_shape=out_shape, in_spec...]
where the time goes in v5:
time: 97.9 us; the launch traced here: 97 us
  Pallas kernels  96.3 us (98%)
    pallas_call x1, Pallas kernels, train(): pl.pallas_call(step_kernel, out_shape=[jax.ShapeDtypeStruct((GROUPS, 2, L...  91.9 us
    pallas_call x1, Pallas kernels, update(): pl.pallas_call(update_kernel, grid=(steps,), out_shape=out_shape, in_spec...  4.35 us

profile of v5, /device:TPU:1, one launch (start us, length us, event | category | flops | bytes accessed | tf_op | source)
XLA Modules:
  0.0 97.0 jit_solution(15176224780350331563)
XLA Ops:
  0.6 91.9 %step.1 = (bf16[8,2,128,128]{3,2,1,0:T(8,128)(2,1)}, f32[4096,128]{1,0:T(8,128)}) custom-call(s32[16,128]{1,0:T(8,128)} %bitcast.24, s32[16,128]{1,0:T(8,128)} %bitcast.25, s32[8,128]{1,0:T(8,128)} %bitcast.27, s32[8,128]{1,0:T(8,128)} %bitcast.28, bf16[128,128]{1,0:T(8,128)(2,1)} %bottom_hbm.1, f32[1,128]{1,0:T(1,128)} %bitcast.29, ...), custom_call_target="tpu_custom_call" | custom-call | tf_op jit(solution)/shard_map/step/pallas_call | solution.py:515
  92.5 4.4 %update.1 = (f32[2048,128]{1,0:T(8,128)}, f32[2,8,128]{2,1,0:T(8,128)}, f32[4096,128]{1,0:T(8,128)}, f32[2,16,128]{2,1,0:T(8,128)}) custom-call(bf16[2048,128]{1,0:T(8,128)(2,1)} %bitcast.22, f32[2,8,128]{2,1,0:T(8,128)} %bitcast.26, f32[2048,128]{1,0:T(8,128)} %hot_table.1, f32[4096,128]{1,0:T(8,128)} %get-tuple-element.11.cold_grad, ...), custom_call_target="tpu_custom_call" | custom-call | tf_op jit(solution)/shard_map/update/pallas_call | solution.py:593

commit v6 on v5

--- a/solution.py
+++ b/solution.py
@@ -241,23 +241,6 @@
     lax.fori_loop(1, MEMBERS, serve_cold, 0)
     pick(cold_table, cold_index, 0, 0, cold_rows.at[me])
 
-    for copy in index_loads + small:
-        copy.wait()
-    unroll = 16
-    drain(hot_rows, 0, MEMBERS - 1, send_sem.at[2], recv_sem.at[2]).wait_recv()
-    hot_wide[...] = hot_rows[...].astype(jnp.float32).reshape(hot_wide.shape)
-    for table in range(TABLES):
-
-        def combine_hot(k, unused):
-            for j in range(unroll):
-                b = k * unroll + j
-                pooled[table, pl.ds(b, 1), :] = (
-                    hot_wide[pl.ds(hot_at[2 * table, b], 1), :]
-                    + hot_wide[pl.ds(hot_at[2 * table + 1, b], 1), :]
-                )
-            return unused
-
-        lax.fori_loop(0, LANES // unroll, combine_hot, 0)
     row_id = lax.broadcasted_iota(jnp.int32, (LANES, LANES), 0)
     lane_id = lax.broadcasted_iota(jnp.int32, (LANES, LANES), 1)
     diagonal = row_id == lane_id
@@ -274,21 +257,39 @@
         for q in range(CLASSES):
             mask[q, n] = jnp.where(wide == q, 1.0, 0.0).astype(jnp.bfloat16)
 
-    def note_hot(i, unused):
-        for c in range(HCAP // LANES):
-            asked = hot_asked[i][:, c * LANES : (c + 1) * LANES]
-            note(asked, HOT_CLASS, i * (HCAP // LANES) + c, hot_ids, hot_mask)
+    together = 4
+
+    def note_some(step, unused):
+        for j in range(together):
+            n = step * together + j
+            asked = hot_asked[step * (together // 2) + j // 2]
+            asked = asked[:, j % 2 * LANES : (j % 2 + 1) * LANES]
+            note(asked, HOT_CLASS, n, hot_ids, hot_mask)
+            asked = cold_asked[4 * n]
+            for q in range(1, 4):
+                asked = jnp.where(quarter == q, cold_asked[4 * n + q], asked)
+            note(asked, COLD_CLASS, n, cold_ids, cold_mask)
         return unused
 
-    def note_cold(n, unused):
-        asked = cold_asked[4 * n]
-        for q in range(1, 4):
-            asked = jnp.where(quarter == q, cold_asked[4 * n + q], asked)
-        note(asked, COLD_CLASS, n, cold_ids, cold_mask)
-        return unused
-
-    lax.fori_loop(0, MEMBERS, note_hot, 0)
-    lax.fori_loop(0, DEVICES // 4, note_cold, 0)
+    lax.fori_loop(0, DEVICES // 4 // together, note_some, 0)
+
+    for copy in index_loads + small:
+        copy.wait()
+    unroll = 16
+    drain(hot_rows, 0, MEMBERS - 1, send_sem.at[2], recv_sem.at[2]).wait_recv()
+    hot_wide[...] = hot_rows[...].astype(jnp.float32).reshape(hot_wide.shape)
+    for table in range(TABLES):
+
+        def combine_hot(k, unused):
+            for j in range(unroll):
+                b = k * unroll + j
+                pooled[table, pl.ds(b, 1), :] = (
+                    hot_wide[pl.ds(hot_at[2 * table, b], 1), :]
+                    + hot_wide[pl.ds(hot_at[2 * table + 1, b], 1), :]
+                )
+            return unused
+
+        lax.fori_loop(0, LANES // unroll, combine_hot, 0)
     drain(cold_rows, 0, DEVICES - 1, send_sem.at[3], recv_sem.at[3]).wait_recv()
     cold_wide[...] = cold_rows[...].astype(jnp.float32).reshape(cold_wide.shape)
     for table in range(TABLES):

time: 97.9 us -> 90.6 us (0.925)
  Pallas kernels: 96.3 us -> 89.8 us
    pallas_call x1, Pallas kernels: 91.9 us -> 85.4 us  [train(): pl.pallas_call(step_kernel, out_shape=[jax.ShapeDtypeStruct((GROUPS, 2, L...]
where the time goes in v6:
time: 90.6 us; the launch traced here: 90.5 us
  Pallas kernels  89.8 us (99%)
    pallas_call x1, Pallas kernels, train(): pl.pallas_call(step_kernel, out_shape=[jax.ShapeDtypeStruct((GROUPS, 2, L...  85.4 us
    pallas_call x1, Pallas kernels, update(): pl.pallas_call(update_kernel, grid=(steps,), out_shape=out_shape, in_spec...  4.35 us

profile of v6, /device:TPU:1, one launch (start us, length us, event | category | flops | bytes accessed | tf_op | source)
XLA Modules:
  0.0 90.5 jit_solution(9101042064199613190)
XLA Ops:
  0.6 85.4 %step.1 = (bf16[8,2,128,128]{3,2,1,0:T(8,128)(2,1)}, f32[4096,128]{1,0:T(8,128)}) custom-call(s32[16,128]{1,0:T(8,128)} %bitcast.24, s32[16,128]{1,0:T(8,128)} %bitcast.25, s32[8,128]{1,0:T(8,128)} %bitcast.27, s32[8,128]{1,0:T(8,128)} %bitcast.28, bf16[128,128]{1,0:T(8,128)(2,1)} %bottom_hbm.1, f32[1,128]{1,0:T(1,128)} %bitcast.29, ...), custom_call_target="tpu_custom_call" | custom-call | tf_op jit(solution)/shard_map/step/pallas_call | solution.py:516
  86.0 4.4 %update.1 = (f32[2048,128]{1,0:T(8,128)}, f32[2,8,128]{2,1,0:T(8,128)}, f32[4096,128]{1,0:T(8,128)}, f32[2,16,128]{2,1,0:T(8,128)}) custom-call(bf16[2048,128]{1,0:T(8,128)(2,1)} %bitcast.22, f32[2,8,128]{2,1,0:T(8,128)} %bitcast.26, f32[2048,128]{1,0:T(8,128)} %hot_table.1, f32[4096,128]{1,0:T(8,128)} %get-tuple-element.11.cold_grad, ...), custom_call_target="tpu_custom_call" | custom-call | tf_op jit(solution)/shard_map/update/pallas_call | solution.py:594
